TPU v7x, 32 devices: a whole 2x2x4 slice. The times are simulated.
32 devices in a mesh: space: 8 (over z, y), view: 4 (over x, core).
Axes of the slice: x: 2, y: 2, z: 4, core: 2. Of those that a mesh axis runs over, the one named last changes fastest.
Arguments:
- gaussians: float32 [59, 65536], P(None, 'space'), as said below
- camera_table: float32 [16, 8], replicated, as said below
- view_camera: int32 [4], P('view'), may hold values from 0 to 15
- tile_plan: int32 [4, 128], P('view', 'space'), may hold values from 2204 to 2595, as said below
- requests: int32 [4, 8, 8, 1024], P('view', 'space'), may hold values from 0 to 8191, as said below
- tile_lists: int32 [4, 128, 512], P('view', 'space'), may hold values from 0 to 8191, as said below
- tile_lengths: int32 [4, 128], P('view', 'space'), may hold values from 128 to 512, as said below
- pixel_grad: float32 [4, 128, 3, 256], P('view', 'space'), may hold values from -0.625 to 0.625
Outputs:
- rendered: float32 [4, 128, 3, 256], P('view', 'space')
- gaussian_grad: float32 [59, 65536], P(None, 'space')
Inputs may be any that keep to these rules, and one draw needn't show every extreme that they name: `tile_plan`: tile ids count 120 tiles to a row; within a view every tile k < 128 of tile row 18 + floor(k / 32) and tile column 44 + (k mod 32) appears exactly once. `requests`: slots of the owner's 8192 Gaussians; within a view no slot of an owner is requested twice, by one renderer or by two. `tile_lists`: position o * 1024 + k names the k-th slot the renderer requested of owner o; the lists of one renderer's tiles together name each of its requested rows exactly once, each list the same number of rows of every owner, ordered by owner and within an owner by slot; entries from the tile's length on are padding. `tile_lengths`: every view has a tile with all 512 entries live. `camera_table`: quaternion rows lead with 2 to 3 and the rest within 0.3; offsets lie within 0.2 across and 4 to 5 in depth; focal lengths 1.8 to 2.4. `gaussians`: the first quaternion entry lies in 1 to 2.
All inputs are finite; a program needn't handle non-finite values.
Results may differ from a plain program's by a relative error of at most 0.0003.
Values sent between devices are 32-bit elements; how exact they have to be, the bound alone decides.
A program may use at most 256 MiB of HBM per device.

v0:
```python
import jax
import jax.numpy as jnp
from jax import lax
from jax.sharding import PartitionSpec as P

sh_zero = 0.28209479177387814
sh_one = 0.4886025119029199
sh_two = (
    1.0925484305920792,
    -1.0925484305920792,
    0.31539156525252005,
    -1.0925484305920792,
    0.5462742152960396,
)
sh_three = (
    -0.5900435899266435,
    2.890611442640554,
    -0.4570457994644658,
    0.3731763325901154,
    -0.4570457994644658,
    1.445305721320277,
    -0.5900435899266435,
)
dilation = 0.3 / 291600.0
highest = lax.Precision.HIGHEST


def quat_matrix(quat_w, quat_x, quat_y, quat_z):
    length = jnp.sqrt(quat_w * quat_w + quat_x * quat_x + quat_y * quat_y + quat_z * quat_z)
    unit_w = quat_w / length
    unit_x = quat_x / length
    unit_y = quat_y / length
    unit_z = quat_z / length
    return [
        [
            1.0 - 2.0 * (unit_y * unit_y + unit_z * unit_z),
            2.0 * (unit_x * unit_y - unit_w * unit_z),
            2.0 * (unit_x * unit_z + unit_w * unit_y),
        ],
        [
            2.0 * (unit_x * unit_y + unit_w * unit_z),
            1.0 - 2.0 * (unit_x * unit_x + unit_z * unit_z),
            2.0 * (unit_y * unit_z - unit_w * unit_x),
        ],
        [
            2.0 * (unit_x * unit_z - unit_w * unit_y),
            2.0 * (unit_y * unit_z + unit_w * unit_x),
            1.0 - 2.0 * (unit_x * unit_x + unit_y * unit_y),
        ],
    ]


def sh_basis(dir_x, dir_y, dir_z):
    sq_x = dir_x * dir_x
    sq_y = dir_y * dir_y
    sq_z = dir_z * dir_z
    return [
        sh_zero * jnp.ones_like(dir_x),
        -sh_one * dir_y,
        sh_one * dir_z,
        -sh_one * dir_x,
        sh_two[0] * dir_x * dir_y,
        sh_two[1] * dir_y * dir_z,
        sh_two[2] * (2.0 * sq_z - sq_x - sq_y),
        sh_two[3] * dir_x * dir_z,
        sh_two[4] * (sq_x - sq_y),
        sh_three[0] * dir_y * (3.0 * sq_x - sq_y),
        sh_three[1] * dir_x * dir_y * dir_z,
        sh_three[2] * dir_y * (4.0 * sq_z - sq_x - sq_y),
        sh_three[3] * dir_z * (2.0 * sq_z - 3.0 * sq_x - 3.0 * sq_y),
        sh_three[4] * dir_x * (4.0 * sq_z - sq_x - sq_y),
        sh_three[5] * dir_z * (sq_x - sq_y),
        sh_three[6] * dir_x * (sq_x - 3.0 * sq_y),
    ]


def project(params, camera):
    center = [params[0], params[1], params[2]]
    scales = [jnp.exp(params[3]), jnp.exp(params[4]), jnp.exp(params[5])]
    own_rot = quat_matrix(params[6], params[7], params[8], params[9])
    view_rot = quat_matrix(camera[0], camera[1], camera[2], camera[3])
    offset_cam = [camera[4], camera[5], camera[6]]
    focal_len = camera[7]
    in_camera = [
        sum((view_rot[i][j] * center[j] for j in range(3))) + offset_cam[i] for i in range(3)
    ]
    shaped = [[own_rot[i][k] * scales[k] for k in range(3)] for i in range(3)]
    turned = [
        [sum((view_rot[i][j] * shaped[j][k] for j in range(3))) for k in range(3)] for i in range(3)
    ]
    inv_depth = 1.0 / in_camera[2]
    screen_u = focal_len * in_camera[0] * inv_depth
    screen_v = focal_len * in_camera[1] * inv_depth
    jac_u = [
        focal_len * inv_depth * turned[0][k] - screen_u * inv_depth * turned[2][k] for k in range(3)
    ]
    jac_v = [
        focal_len * inv_depth * turned[1][k] - screen_v * inv_depth * turned[2][k] for k in range(3)
    ]
    cov_uu = sum((jac_u[k] * jac_u[k] for k in range(3))) + dilation
    cov_uv = sum((jac_u[k] * jac_v[k] for k in range(3)))
    cov_vv = sum((jac_v[k] * jac_v[k] for k in range(3))) + dilation
    determinant = cov_uu * cov_vv - cov_uv * cov_uv
    opacity = jax.nn.sigmoid(params[10])
    eye_pos = [-sum((view_rot[j][i] * offset_cam[j] for j in range(3))) for i in range(3)]
    toward = [center[i] - eye_pos[i] for i in range(3)]
    length = jnp.sqrt(toward[0] * toward[0] + toward[1] * toward[1] + toward[2] * toward[2])
    basis = sh_basis(toward[0] / length, toward[1] / length, toward[2] / length)
    colors = [0.5 + sum((basis[k] * params[11 + 3 * k + h] for k in range(16))) for h in range(3)]
    return jnp.stack(
        [
            screen_u,
            screen_v,
            cov_vv / determinant,
            -cov_uv / determinant,
            cov_uu / determinant,
            opacity,
        ]
        + colors
    )


def pixel_points(tile_ids):
    pixel = jnp.arange(256, dtype=jnp.int32)[None, :]
    column = tile_ids[:, None] % 120 * 16 + pixel % 16
    row_at = tile_ids[:, None] // 120 * 16 + pixel // 16
    point_u = (column.astype(jnp.float32) + 0.5 - 960.0) / 540.0
    point_v = (row_at.astype(jnp.float32) + 0.5 - 540.0) / 540.0
    return (point_u, point_v)


def block_alpha(cols, point_u, point_v, lengths):
    width = cols.shape[2]
    diff_u = point_u[:, :, None] - cols[0][:, None, :]
    diff_v = point_v[:, :, None] - cols[1][:, None, :]
    power = -0.5 * (
        cols[2][:, None, :] * diff_u * diff_u
        + 2.0 * cols[3][:, None, :] * diff_u * diff_v
        + cols[4][:, None, :] * diff_v * diff_v
    )
    alpha = cols[5][:, None, :] * jnp.exp(power)
    alive = jnp.arange(width, dtype=jnp.int32)[None, :] < lengths[:, None]
    return jnp.where(alive[:, None, :], alpha, 0.0)


def triangle(width):
    return (
        lax.broadcasted_iota(jnp.int32, (width, width), 0)
        < lax.broadcasted_iota(jnp.int32, (width, width), 1)
    ).astype(jnp.float32)


def composite(features, entries, lengths, tile_ids):
    tile_count, span = entries.shape
    columns = jnp.take(features, entries.reshape(-1), axis=1).reshape(
        features.shape[0], tile_count, span
    )
    point_u, point_v = pixel_points(tile_ids)
    alpha = block_alpha(columns, point_u, point_v, lengths)
    logs = jnp.log1p(-alpha)
    before = jnp.einsum("tpk,kj->tpj", logs, triangle(span), precision=highest)
    weights = alpha * jnp.exp(before)
    return jnp.einsum("ctk,tpk->tcp", columns[6:9], weights, precision=highest)


def per_device(
    gaussians, camera_table, view_camera, tile_plan, requests, tile_lists, tile_lengths, pixel_grad
):
    table_rows = camera_table.shape[0]
    chosen = (jnp.arange(table_rows, dtype=jnp.int32) == view_camera[0]).astype(jnp.float32)
    camera = jnp.sum(camera_table * chosen[:, None], axis=0)
    wanted = requests[0, 0].reshape(-1)
    incoming = lax.all_to_all(wanted, "space", split_axis=0, concat_axis=0, tiled=True)

    def draw_image(features):
        return composite(features, tile_lists[0], tile_lengths[0], tile_plan[0])

    outgoing = jnp.take(gaussians, incoming, axis=1)
    arrived = lax.all_to_all(outgoing, "space", split_axis=1, concat_axis=1, tiled=True)

    def draw_from_params(params):
        return draw_image(project(params, camera))

    image, back_render = jax.vjp(draw_from_params, arrived)
    (row_grad,) = back_render(pixel_grad[0])
    returned = lax.all_to_all(row_grad, "space", split_axis=1, concat_axis=1, tiled=True)
    local_grad = jnp.zeros_like(gaussians).at[:, incoming].add(returned)
    total = lax.psum(local_grad, "view")
    return (image[None], total)


def solution(mesh):
    placed = (
        P(None, "space"),
        P(),
        P("view"),
        P("view", "space"),
        P("view", "space", None, None),
        P("view", "space", None),
        P("view", "space"),
        P("view", "space", None, None),
    )
    return jax.shard_map(
        per_device,
        mesh=mesh,
        in_specs=placed,
        out_specs=(P("view", "space", None, None), P(None, "space")),
        check_vma=False,
    )
```

profile of v0, /device:TPU:0, one launch (start us, length us, event | category | flops | bytes accessed | tf_op | source)
XLA Modules:
  0.0 553.5 jit_solution(9596229358758484810)
XLA Ops:
  7.2 1.4 all_to_all.22
  8.6 7.3 %all-to-all-start = ((s32[8,1024,1]{1,2,0:T(1,128)}), s32[8,1024,1]{1,2,0:T(1,128)S(1)}, u32[]{:S(2)}, u32[]{:S(2)}) async-start(s32[8,1024,1]{1,2,0:T(1,128)} %all_to_all.22), calls=%async_computation | async-start | bytes 65536 | tf_op jit(solution)/shard_map/all_to_all | solution.py:173
  16.5 3.9 copy.441
  20.4 2.1 all-to-all-done
  22.6 29.9 %gather_fusion = f32[8192,59]{1,0:T(8,128)} fusion(f32[59,8192]{0,1:T(8,128)} %copy.441, s32[8192]{0:T(1024)S(1)} %broadcast_clamp_fusion.1), kind=kCustom, calls=%fused_computation | custom fusion | bytes 3899392 | tf_op jit(solution)/shard_map/jit(_take)/gather | solution.py:178
  52.5 2.9 copy.442
  55.5 1.6 broadcast_select_fusion
  57.0 3.9 all-to-all-start.1
  78.7 29.9 %all-to-all-done.1 = f32[59,8,1024]{2,0,1:T(8,128)S(1)} async-done(((f32[59,8,1024]{2,0,1:T(8,128)}), f32[59,8,1024]{2,0,1:T(8,128)S(1)}, u32[]{:S(2)}, u32[]{:S(2)}) %all-to-all-start.1) | async-done | bytes 1933344 | tf_op jit(solution)/shard_map/all_to_all | solution.py:179
  109.9 3.2 divide_bitcast_fusion
  114.1 3.0 fusion.115
  118.0 1.4 add_add_fusion.18
  121.3 2.0 stack.2
  123.2 2.7 copy.447
  126.0 29.9 %gather_fusion.1 = f32[8192,9]{1,0:T(8,128)} fusion(f32[9,8192]{0,1:T(8,128)} %copy.447, s32[8192]{0:T(1024)S(1)} %copy-done.86), kind=kCustom, calls=%fused_computation.1 | custom fusion | bytes 622592 | tf_op jit(solution)/shard_map/jvp(jit(_take))/gather | solution.py:155
  155.9 3.0 copy.448
  160.4 13.8 %fusion.21 = f32[16,256,512]{2,1,0:T(8,128)S(1)} fusion(f32[16,512]{1,0:T(8,128)S(1)} %mul.10814, f32[16,512]{1,0:T(8,128)S(1)} %sub.1658, f32[16,256]{1,0:T(8,128)S(1)} %copy-done.104, f32[16,512]{1,0:T(8,128)S(1)} %mul.10809, f32[16,512]{1,0:T(8,128)S(1)} %sub.1650, f32[16,256]{1,0:T(8,128)S(1)} %copy-done.106, f32[16,512]{1,0:T(8,128)S(1)} %mul.10803, ...), kind=kOutput, calls=%fused_computation.39 | convolution fusion | flops 12914524160 | bytes 8626176 | tf_op jit(solution)/shard_map/jvp(tpk,kj->tpj)/dot_general | solution.py:161
  174.2 10.9 %fusion.41 = f32[3,16,512]{2,0,1:T(4,128)S(1)} fusion(f32[16,256,512]{2,1,0:T(8,128)S(1)} %fusion.21, f32[16,512]{1,0:T(8,128)S(1)} %mul.10814, f32[16,512]{1,0:T(8,128)S(1)} %sub.1658, f32[16,256]{1,0:T(8,128)S(1)} %copy-done.104, f32[16,512]{1,0:T(8,128)S(1)} %mul.10809, f32[16,512]{1,0:T(8,128)S(1)} %sub.1650, f32[16,256]{1,0:T(8,128)S(1)} %copy-done.106, ...), kind=kOutput, calls=%fused_computation.58 | convolution fusion | flops 104857600 | bytes 8773632 | tf_op jit(solution)/shard_map/transpose(jvp(ctk,tpk->tcp))/dot_general | solution.py:163
  185.1 6.8 %fusion.46 = f32[16,512,256]{1,2,0:T(8,128)S(1)} fusion(f32[3,16,512]{2,0,1:T(4,128)S(1)} %bitcast.218, f32[16,3,256]{2,0,1:T(8,128)S(1)} %bitcast.167), kind=kOutput, calls=%fused_computation.69 | convolution fusion | flops 75497472 | bytes 8536064 | tf_op jit(solution)/shard_map/transpose(jvp(ctk,tpk->tcp))/dot_general | solution.py:163
  191.9 26.5 %fusion.13 = (f32[16,512]{1,0:T(8,128)S(1)}, f32[16,512]{1,0:T(8,128)S(1)}, f32[16,512]{1,0:T(8,128)S(1)}, f32[16,512]{1,0:T(8,128)S(1)}, f32[16,512]{1,0:T(8,128)S(1)}, /*index=5*/f32[16,512]{1,0:T(8,128)S(1)}) fusion(f32[16,512]{1,0:T(8,128)S(1)} %sub.1658, f32[16,256]{1,0:T(8,128)S(1)} %copy-done.104, f32[16,512]{1,0:T(8,128)S(1)} %mul.10814, ...), kind=kOutput, calls=%fused_computation.28 | convolution fusion | flops 13010944000 | bytes 17211392 | tf_op jit(solution)/shard_map/transpose(jvp(tpk,kj->tpj))/dot_general | solution.py:161
  219.6 2.7 copy.454
  222.2 46.6 %scatter_custom_fusion = f32[9,8192]{0,1:T(8,128)} fusion(s32[8192]{0:T(1024)} %bitcast.329, f32[8192,9]{1,0:T(8,128)} %copy.454, f32[]{:T(128)} %constant.73.clone.1), kind=kCustom, calls=%fused_computation.54 | custom fusion | flops 73728 | bytes 295424 | tf_op jit(solution)/shard_map/transpose(jvp(jit(_take)))/scatter-add | solution.py:155
  268.8 33.8 %fusion.116 = (f32[1,8192]{0,1:T(8,128)}, f32[1,8192]{0,1:T(8,128)}, f32[1,8192]{0,1:T(8,128)}, f32[1,8192]{0,1:T(8,128)}, f32[1,8192]{0,1:T(8,128)}, /*index=5*...) fusion(f32[9,8192]{0,1:T(8,128)} %scatter_custom_fusion), kind=kLoop, calls=%fused_computation.341 | loop fusion | bytes 589824 | tf_op jit(solution)/shard_map/transpose(jvp())/unstack | solution.py:110
  302.6 2.8 copy.477
  306.1 2.8 copy.474
  309.0 2.8 copy.476
  311.8 2.8 copy.475
  314.7 2.8 copy.481
  317.5 2.8 copy.480
  320.4 2.8 copy.479
  323.2 2.9 copy.478
  326.1 2.9 copy.482
  329.5 1.1 multiply_add_fusion.34
  331.6 2.4 add_add_fusion.12
  334.0 1.4 add_add_fusion.9
  335.8 2.6 fusion.111
  339.8 4.7 multiply_add_fusion.7
  345.8 5.3 pad_add_fusion
  351.2 1.3 copy.494
  352.6 1.1 copy.464
  353.8 51.8 %all_to_all.33 = f32[59,8,1024]{2,0,1:T(8,128)S(1)} all-to-all(f32[59,8,1024]{2,0,1:T(8,128)S(1)} %copy.464), channel_id=1, replica_groups=mesh['space'=8,'view'=4] {'space'}, dimensions={1} | all-to-all | bytes 3866624 | tf_op jit(solution)/shard_map/all_to_all | solution.py:186
  405.6 1.1 copy.465
  407.0 1.2 copy.495
  408.2 2.8 copy.466
  411.1 46.6 %scatter_custom_fusion.1 = f32[59,8192]{0,1:T(8,128)} fusion(s32[8192]{0:T(1024)} %bitcast.327, f32[8192,59]{1,0:T(8,128)} %copy.466, f32[]{:T(128)} %constant.73.clone.1), kind=kCustom, calls=%fused_computation.56 | custom fusion | flops 483328 | bytes 1933824 | tf_op jit(solution)/shard_map/scatter-add | solution.py:187
  457.8 13.9 %fusion.42 = f32[1,16,3,256]{3,2,1,0:T(4,128)S(1)} fusion(f32[3,16,512]{2,0,1:T(4,128)S(1)} %bitcast.219, f32[16,256,512]{2,1,0:T(8,128)} %copy-done.113, f32[16,512]{1,0:T(8,128)S(1)} %copy-done.95, f32[16,512]{1,0:T(8,128)S(1)} %copy-done.97, f32[16,256]{1,0:T(8,128)S(1)} %copy-done.105, f32[16,512]{1,0:T(8,128)S(1)} %copy-done.99, ...), kind=kOutput, calls=%fused_computation.59 | convolution fusion | flops 104857600 | bytes 8773632 | tf_op jit(solution)/shard_map/jvp(ctk,tpk->tcp)/dot_general | solution.py:163
  472.4 70.0 %all-reduce.68.cloned.1.call-done = f32[59,8192]{0,1:T(8,128)} async-done(((f32[59,8192]{0,1:T(8,128)}), f32[59,8192]{0,1:T(8,128)}) %all-reduce.68.cloned.1.call-update) | async-done | bytes 1933328 | tf_op jit(solution)/shard_map/psum | solution.py:188
  542.4 3.8 copy.468
  (297 shorter events, 16.8 us)
Async XLA Ops:
  7.2 167.0 %copy-start = (f32[1,16,3,256]{3,1,2,0:T(8,128)S(1)}, f32[1,16,3,256]{3,1,2,0:T(8,128)}, u32[]{:S(2)}) copy-start(f32[1,16,3,256]{3,1,2,0:T(8,128)} %param.15) | copy-start | bytes 147460
  8.6 14.0 %all-to-all-start = ((s32[8,1024,1]{1,2,0:T(1,128)}), s32[8,1024,1]{1,2,0:T(1,128)S(1)}, u32[]{:S(2)}, u32[]{:S(2)}) async-start(s32[8,1024,1]{1,2,0:T(1,128)} %all_to_all.22), calls=%async_computation | async-start | bytes 65536 | tf_op jit(solution)/shard_map/all_to_all | solution.py:173
  22.6 29.9 %copy-start.88 = (s32[8192,1]{0,1:T(1,128)}, s32[8192,1]{0,1:T(1,128)S(1)}, u32[]{:S(2)}) copy-start(s32[8192,1]{0,1:T(1,128)S(1)} %compare_select_fusion.1) | copy-start | bytes 98308
  55.4 19.9 %copy-start.87 = (s32[1,16,512]{2,1,0:T(8,128)S(1)}, s32[1,16,512]{2,1,0:T(8,128)}, u32[]{:S(2)}) copy-start(s32[1,16,512]{2,1,0:T(8,128)} %param.13) | copy-start | bytes 98308
  55.5 20.0 %copy-start.112 = (s32[1,16]{1,0:T(1,128)S(1)}, s32[1,16]{1,0:T(1,128)}, u32[]{:S(2)}) copy-start(s32[1,16]{1,0:T(1,128)} %param.11) | copy-start | bytes 196
  55.5 20.0 %copy-start.111 = (s32[1,16]{1,0:T(1,128)S(1)}, s32[1,16]{1,0:T(1,128)}, u32[]{:S(2)}) copy-start(s32[1,16]{1,0:T(1,128)} %param.14) | copy-start | bytes 196
  57.0 51.6 %all-to-all-start.1 = ((f32[59,8,1024]{2,0,1:T(8,128)}), f32[59,8,1024]{2,0,1:T(8,128)S(1)}, u32[]{:S(2)}, u32[]{:S(2)}) async-start(f32[59,8,1024]{2,0,1:T(8,128)} %broadcast_select_fusion), calls=%async_computation.1 | async-start | bytes 4194304 | tf_op jit(solution)/shard_map/all_to_all | solution.py:179
  60.9 481.5 %all-reduce.68.cloned.1.call-start = ((), (), s32[]{:S(2)}) async-start(), calls=%async_computation.3 | async-start | bytes 8388608 | tf_op jit(solution)/shard_map/psum | solution.py:188
  120.1 35.7 %copy-start.4 = (f32[1,8,1024]{2,0,1:T(1,128)}, f32[1,8,1024]{2,0,1:T(1,128)S(1)}, u32[]{:S(2)}) copy-start(f32[1,8,1024]{2,0,1:T(1,128)S(1)} %get-tuple-element.151) | copy-start | bytes 98308
  120.1 35.7 %copy-start.6 = (f32[1,8,1024]{2,0,1:T(1,128)}, f32[1,8,1024]{2,0,1:T(1,128)S(1)}, u32[]{:S(2)}) copy-start(f32[1,8,1024]{2,0,1:T(1,128)S(1)} %get-tuple-element.152) | copy-start | bytes 98308
  120.1 35.7 %copy-start.8 = (f32[1,8,1024]{2,0,1:T(1,128)}, f32[1,8,1024]{2,0,1:T(1,128)S(1)}, u32[]{:S(2)}) copy-start(f32[1,8,1024]{2,0,1:T(1,128)S(1)} %get-tuple-element.153) | copy-start | bytes 98308
  126.0 33.0 %copy-start.91 = (pred[8192]{0:T(1024)(128)(4,1)S(1)}, pred[8192]{0:T(1024)(128)(4,1)}, u32[]{:S(2)}) copy-start(pred[8192]{0:T(1024)(128)(4,1)} %compare_and_fusion.1) | copy-start | bytes 24580
  160.2 31.6 %copy-start.92 = (f32[16,512]{1,0:T(8,128)}, f32[16,512]{1,0:T(8,128)S(1)}, u32[]{:S(2)}) copy-start(f32[16,512]{1,0:T(8,128)S(1)} %mul.10801) | copy-start | bytes 98308
  160.2 31.6 %copy-start.94 = (f32[16,512]{1,0:T(8,128)}, f32[16,512]{1,0:T(8,128)S(1)}, u32[]{:S(2)}) copy-start(f32[16,512]{1,0:T(8,128)S(1)} %mul.10814) | copy-start | bytes 98308
  160.3 31.6 %copy-start.96 = (f32[16,512]{1,0:T(8,128)}, f32[16,512]{1,0:T(8,128)S(1)}, u32[]{:S(2)}) copy-start(f32[16,512]{1,0:T(8,128)S(1)} %sub.1658) | copy-start | bytes 98308
  160.3 31.6 %copy-start.98 = (f32[16,512]{1,0:T(8,128)}, f32[16,512]{1,0:T(8,128)S(1)}, u32[]{:S(2)}) copy-start(f32[16,512]{1,0:T(8,128)S(1)} %mul.10809) | copy-start | bytes 98308
  160.3 31.5 %copy-start.100 = (f32[16,512]{1,0:T(8,128)}, f32[16,512]{1,0:T(8,128)S(1)}, u32[]{:S(2)}) copy-start(f32[16,512]{1,0:T(8,128)S(1)} %sub.1650) | copy-start | bytes 98308
  160.3 31.5 %copy-start.102 = (f32[16,512]{1,0:T(8,128)}, f32[16,512]{1,0:T(8,128)S(1)}, u32[]{:S(2)}) copy-start(f32[16,512]{1,0:T(8,128)S(1)} %mul.10803) | copy-start | bytes 98308
  174.2 17.7 %copy-start.113 = (f32[16,256,512]{2,1,0:T(8,128)}, f32[16,256,512]{2,1,0:T(8,128)S(1)}, u32[]{:S(2)}) copy-start(f32[16,256,512]{2,1,0:T(8,128)S(1)} %fusion.21) | copy-start | bytes 25165828
  328.9 10.5 %copy-start.3 = (f32[1,8192]{1,0:T(1,128)S(1)}, f32[1,8192]{1,0:T(1,128)}, u32[]{:S(2)}) copy-start(f32[1,8192]{1,0:T(1,128)} %copy-done.2) | copy-start | bytes 98308
  328.9 10.5 %copy-start.5 = (f32[1,8,1024]{2,0,1:T(1,128)S(1)}, f32[1,8,1024]{2,0,1:T(1,128)}, u32[]{:S(2)}) copy-start(f32[1,8,1024]{2,0,1:T(1,128)} %copy-done.4) | copy-start | bytes 98308
  329.0 10.5 %copy-start.7 = (f32[1,8,1024]{2,0,1:T(1,128)S(1)}, f32[1,8,1024]{2,0,1:T(1,128)}, u32[]{:S(2)}) copy-start(f32[1,8,1024]{2,0,1:T(1,128)} %copy-done.6) | copy-start | bytes 98308
  329.0 10.5 %copy-start.9 = (f32[1,8,1024]{2,0,1:T(1,128)S(1)}, f32[1,8,1024]{2,0,1:T(1,128)}, u32[]{:S(2)}) copy-start(f32[1,8,1024]{2,0,1:T(1,128)} %copy-done.8) | copy-start | bytes 98308
  329.0 10.5 %copy-start.11 = (f32[1,8,1024]{2,0,1:T(1,128)S(1)}, f32[1,8,1024]{2,0,1:T(1,128)}, u32[]{:S(2)}) copy-start(f32[1,8,1024]{2,0,1:T(1,128)} %copy-done.10) | copy-start | bytes 98308
  329.0 10.5 %copy-start.13 = (f32[1,8,1024]{2,0,1:T(1,128)S(1)}, f32[1,8,1024]{2,0,1:T(1,128)}, u32[]{:S(2)}) copy-start(f32[1,8,1024]{2,0,1:T(1,128)} %copy-done.12) | copy-start | bytes 98308
  329.0 10.5 %copy-start.15 = (f32[1,8,1024]{2,0,1:T(1,128)S(1)}, f32[1,8,1024]{2,0,1:T(1,128)}, u32[]{:S(2)}) copy-start(f32[1,8,1024]{2,0,1:T(1,128)} %copy-done.14) | copy-start | bytes 98308
  329.0 10.5 %copy-start.17 = (f32[1,8,1024]{2,0,1:T(1,128)S(1)}, f32[1,8,1024]{2,0,1:T(1,128)}, u32[]{:S(2)}) copy-start(f32[1,8,1024]{2,0,1:T(1,128)} %copy-done.16) | copy-start | bytes 98308
  329.0 10.5 %copy-start.19 = (f32[1,8,1024]{2,0,1:T(1,128)S(1)}, f32[1,8,1024]{2,0,1:T(1,128)}, u32[]{:S(2)}) copy-start(f32[1,8,1024]{2,0,1:T(1,128)} %copy-done.18) | copy-start | bytes 98308
  329.0 10.5 %copy-start.21 = (f32[1,8,1024]{2,0,1:T(1,128)S(1)}, f32[1,8,1024]{2,0,1:T(1,128)}, u32[]{:S(2)}) copy-start(f32[1,8,1024]{2,0,1:T(1,128)} %copy-done.20) | copy-start | bytes 98308
  329.0 10.5 %copy-start.23 = (f32[1,8,1024]{2,0,1:T(1,128)S(1)}, f32[1,8,1024]{2,0,1:T(1,128)}, u32[]{:S(2)}) copy-start(f32[1,8,1024]{2,0,1:T(1,128)} %copy-done.22) | copy-start | bytes 98308
  329.0 10.5 %copy-start.25 = (f32[1,8,1024]{2,0,1:T(1,128)S(1)}, f32[1,8,1024]{2,0,1:T(1,128)}, u32[]{:S(2)}) copy-start(f32[1,8,1024]{2,0,1:T(1,128)} %copy-done.24) | copy-start | bytes 98308
  329.1 10.5 %copy-start.27 = (f32[1,8,1024]{2,0,1:T(1,128)S(1)}, f32[1,8,1024]{2,0,1:T(1,128)}, u32[]{:S(2)}) copy-start(f32[1,8,1024]{2,0,1:T(1,128)} %copy-done.26) | copy-start | bytes 98308
  329.1 10.5 %copy-start.29 = (f32[1,8,1024]{2,0,1:T(1,128)S(1)}, f32[1,8,1024]{2,0,1:T(1,128)}, u32[]{:S(2)}) copy-start(f32[1,8,1024]{2,0,1:T(1,128)} %copy-done.28) | copy-start | bytes 98308
  329.1 10.5 %copy-start.31 = (f32[1,8,1024]{2,0,1:T(1,128)S(1)}, f32[1,8,1024]{2,0,1:T(1,128)}, u32[]{:S(2)}) copy-start(f32[1,8,1024]{2,0,1:T(1,128)} %copy-done.30) | copy-start | bytes 98308
  329.1 10.5 %copy-start.33 = (f32[1,8,1024]{2,0,1:T(1,128)S(1)}, f32[1,8,1024]{2,0,1:T(1,128)}, u32[]{:S(2)}) copy-start(f32[1,8,1024]{2,0,1:T(1,128)} %copy-done.32) | copy-start | bytes 98308
  329.1 10.5 %copy-start.35 = (f32[1,8,1024]{2,0,1:T(1,128)S(1)}, f32[1,8,1024]{2,0,1:T(1,128)}, u32[]{:S(2)}) copy-start(f32[1,8,1024]{2,0,1:T(1,128)} %copy-done.34) | copy-start | bytes 98308
  329.1 10.5 %copy-start.37 = (f32[1,8,1024]{2,0,1:T(1,128)S(1)}, f32[1,8,1024]{2,0,1:T(1,128)}, u32[]{:S(2)}) copy-start(f32[1,8,1024]{2,0,1:T(1,128)} %copy-done.36) | copy-start | bytes 98308
  329.1 10.5 %copy-start.41 = (f32[1,1,8,1024]{3,1,2,0:T(1,128)S(1)}, f32[1,1,8,1024]{3,1,2,0:T(1,128)}, u32[]{:S(2)}) copy-start(f32[1,1,8,1024]{3,1,2,0:T(1,128)} %copy-done.40) | copy-start | bytes 98308
  411.0 46.7 %copy-start.93 = (f32[16,512]{1,0:T(8,128)S(1)}, f32[16,512]{1,0:T(8,128)}, u32[]{:S(2)}) copy-start(f32[16,512]{1,0:T(8,128)} %copy-done.92) | copy-start | bytes 98308
  411.0 46.7 %copy-start.95 = (f32[16,512]{1,0:T(8,128)S(1)}, f32[16,512]{1,0:T(8,128)}, u32[]{:S(2)}) copy-start(f32[16,512]{1,0:T(8,128)} %copy-done.94) | copy-start | bytes 98308
  411.0 46.7 %copy-start.97 = (f32[16,512]{1,0:T(8,128)S(1)}, f32[16,512]{1,0:T(8,128)}, u32[]{:S(2)}) copy-start(f32[16,512]{1,0:T(8,128)} %copy-done.96) | copy-start | bytes 98308
  411.0 46.7 %copy-start.99 = (f32[16,512]{1,0:T(8,128)S(1)}, f32[16,512]{1,0:T(8,128)}, u32[]{:S(2)}) copy-start(f32[16,512]{1,0:T(8,128)} %copy-done.98) | copy-start | bytes 98308
  411.0 46.7 %copy-start.101 = (f32[16,512]{1,0:T(8,128)S(1)}, f32[16,512]{1,0:T(8,128)}, u32[]{:S(2)}) copy-start(f32[16,512]{1,0:T(8,128)} %copy-done.100) | copy-start | bytes 98308
  411.0 46.7 %copy-start.103 = (f32[16,512]{1,0:T(8,128)S(1)}, f32[16,512]{1,0:T(8,128)}, u32[]{:S(2)}) copy-start(f32[16,512]{1,0:T(8,128)} %copy-done.102) | copy-start | bytes 98308
  411.1 46.7 %copy-start.105 = (f32[16,256]{1,0:T(8,128)S(1)}, f32[16,256]{1,0:T(8,128)}, u32[]{:S(2)}) copy-start(f32[16,256]{1,0:T(8,128)} %get-tuple-element.270) | copy-start | bytes 49156
  411.1 46.7 %copy-start.107 = (f32[16,256]{1,0:T(8,128)S(1)}, f32[16,256]{1,0:T(8,128)}, u32[]{:S(2)}) copy-start(f32[16,256]{1,0:T(8,128)} %get-tuple-element.271) | copy-start | bytes 49156
  411.1 46.7 %copy-start.109 = (pred[16,512]{1,0:T(8,128)(4,1)S(1)}, pred[16,512]{1,0:T(8,128)(4,1)}, u32[]{:S(2)}) copy-start(pred[16,512]{1,0:T(8,128)(4,1)} %iota_compare_fusion.1) | copy-start | bytes 24580
  457.8 88.4 %copy-start.1 = (f32[1,16,3,256]{3,1,2,0:T(8,128)S(1)}, f32[1,16,3,256]{3,1,2,0:T(8,128)}, u32[]{:S(2)}) copy-start(f32[1,16,3,256]{3,1,2,0:T(8,128)} %param.15) | copy-start | bytes 147460
  (69 other events, 422.9 us)
Sparse Core Ops, SparseCore 0:
  457.8 84.5 all-reduce.67
where the time goes:
time: 562 us; the launch traced here: 554 us
  local copies, waits for them, and re-layouts  154 us (27%)
  other arithmetic  131 us (23%)
  waiting for transfers between devices  102 us (18%)
  matrix products  71.9 us (13%)
  blocking collectives  51.8 us (9%)
  between operations  30.8 us (5%)
  starting transfers between devices  11.2 us (2%)
    psum x1, waiting for transfers between devices, per_device(): total = lax.psum(local_grad, 'view')  70 us
    all_to_all x1, blocking collectives, per_device(): lax.all_to_all(row_grad, 'space', split_axis=1, concat_axis=1, tiled=True)  51.8 us
    scatter-add x1, other arithmetic, per_device(): local_grad = jnp.zeros_like(gaussians).at[:, incoming].add(returned)  46.6 us
    scatter-add x1, other arithmetic, composite(): jnp.take(features, entries.reshape(-1), axis=1)  46.6 us
    dot_general x2, matrix products, composite(): before = jnp.einsum('tpk,kj->tpj', logs, triangle(span), precision=highest)  40.3 us
    unnamed x255, local copies, waits for them, and re-layouts  39.7 us
    another operation x3, local copies, waits for them, and re-layouts, project(): jnp.stack([screen_u, screen_v, cov_vv / determinant, -cov_uv / determinan...  38.4 us
    gather x2, local copies, waits for them, and re-layouts, composite(): jnp.take(features, entries.reshape(-1), axis=1)  32.9 us
  transfers between devices with their start and end apart: 3, of which 3 were waited for; matrix products, arithmetic and copies ran while one was open for 4% of the time, Pallas kernels for 0%

commit v1 on v0

v1 whole, which is shorter than its diff:
```python
import functools
import math

import jax
import jax.numpy as jnp
import numpy as np
from jax import lax
from jax.experimental import pallas as pl
from jax.experimental.pallas import tpu as pltpu
from jax.sharding import PartitionSpec as P

sh_zero = 0.28209479177387814
sh_one = 0.4886025119029199
sh_two = (
    1.0925484305920792,
    -1.0925484305920792,
    0.31539156525252005,
    -1.0925484305920792,
    0.5462742152960396,
)
sh_three = (
    -0.5900435899266435,
    2.890611442640554,
    -0.4570457994644658,
    0.3731763325901154,
    -0.4570457994644658,
    1.445305721320277,
    -0.5900435899266435,
)
dilation = 0.3 / 291600.0
LOG2E = math.log2(math.e)
HALF = 540.0
F32 = jnp.float32
BF16 = jnp.bfloat16
LANES = 128
VMEM = pl.BlockSpec(memory_space=pltpu.VMEM)


def quat_matrix(quat_w, quat_x, quat_y, quat_z):
    inv = 1.0 / jnp.sqrt(quat_w * quat_w + quat_x * quat_x + quat_y * quat_y + quat_z * quat_z)
    w, x, y, z = quat_w * inv, quat_x * inv, quat_y * inv, quat_z * inv
    return [
        [1.0 - 2.0 * (y * y + z * z), 2.0 * (x * y - w * z), 2.0 * (x * z + w * y)],
        [2.0 * (x * y + w * z), 1.0 - 2.0 * (x * x + z * z), 2.0 * (y * z - w * x)],
        [2.0 * (x * z - w * y), 2.0 * (y * z + w * x), 1.0 - 2.0 * (x * x + y * y)],
    ]


def sh_basis(dir_x, dir_y, dir_z):
    sq_x = dir_x * dir_x
    sq_y = dir_y * dir_y
    sq_z = dir_z * dir_z
    return [
        -sh_one * dir_y,
        sh_one * dir_z,
        -sh_one * dir_x,
        sh_two[0] * dir_x * dir_y,
        sh_two[1] * dir_y * dir_z,
        sh_two[2] * (2.0 * sq_z - sq_x - sq_y),
        sh_two[3] * dir_x * dir_z,
        sh_two[4] * (sq_x - sq_y),
        sh_three[0] * dir_y * (3.0 * sq_x - sq_y),
        sh_three[1] * dir_x * dir_y * dir_z,
        sh_three[2] * dir_y * (4.0 * sq_z - sq_x - sq_y),
        sh_three[3] * dir_z * (2.0 * sq_z - 3.0 * sq_x - 3.0 * sq_y),
        sh_three[4] * dir_x * (4.0 * sq_z - sq_x - sq_y),
        sh_three[5] * dir_z * (sq_x - sq_y),
        sh_three[6] * dir_x * (sq_x - 3.0 * sq_y),
    ]


def geometry(params, camera):
    center = params[0:3]
    scales = [jnp.exp(params[3]), jnp.exp(params[4]), jnp.exp(params[5])]
    own_rot = quat_matrix(*params[6:10])
    view_rot, offset_cam, focal_len = camera
    in_camera = [
        sum((view_rot[i][j] * center[j] for j in range(3))) + offset_cam[i] for i in range(3)
    ]
    shaped = [[own_rot[i][k] * scales[k] for k in range(3)] for i in range(3)]
    turned = [
        [sum((view_rot[i][j] * shaped[j][k] for j in range(3))) for k in range(3)] for i in range(3)
    ]
    inv_depth = 1.0 / in_camera[2]
    screen_u = focal_len * in_camera[0] * inv_depth
    screen_v = focal_len * in_camera[1] * inv_depth
    jac_u = [
        focal_len * inv_depth * turned[0][k] - screen_u * inv_depth * turned[2][k] for k in range(3)
    ]
    jac_v = [
        focal_len * inv_depth * turned[1][k] - screen_v * inv_depth * turned[2][k] for k in range(3)
    ]
    cov_uu = sum((jac_u[k] * jac_u[k] for k in range(3))) + dilation
    cov_uv = sum((jac_u[k] * jac_v[k] for k in range(3)))
    cov_vv = sum((jac_v[k] * jac_v[k] for k in range(3))) + dilation
    inv_det = 1.0 / (cov_uu * cov_vv - cov_uv * cov_uv)
    return [screen_u, screen_v, cov_vv * inv_det, -cov_uv * inv_det, cov_uu * inv_det]


def directional(center, camera):
    view_rot, offset_cam, _ = camera
    toward = [
        center[i] + sum((view_rot[j][i] * offset_cam[j] for j in range(3))) for i in range(3)
    ]
    inv = 1.0 / jnp.sqrt(toward[0] * toward[0] + toward[1] * toward[1] + toward[2] * toward[2])
    return sh_basis(toward[0] * inv, toward[1] * inv, toward[2] * inv)


def unpack_camera(rows):
    full = [jnp.broadcast_to(rows[i : i + 1], (8, LANES)) for i in range(8)]
    return (quat_matrix(*full[0:4]), full[4:7], full[7])


def project_kernel(params_ref, camera_ref, out_ref):
    camera = unpack_camera(camera_ref[...])
    params = [params_ref[i] for i in range(11)]
    feats = geometry(params, camera)
    logit = params[10]
    feats.append(jnp.minimum(logit, 0.0) - jnp.log1p(jnp.exp(-jnp.abs(logit))))
    basis = directional(params[0:3], camera)
    for h in range(3):
        total = 0.5 + sh_zero * params_ref[11 + h]
        for k in range(1, 16):
            total = total + basis[k - 1] * params_ref[11 + 3 * k + h]
        feats.append(total)
    for i in range(9):
        out_ref[i] = feats[i]


def project_all(params, camera):
    blocks = params.shape[1] // 8
    return pl.pallas_call(
        project_kernel,
        grid=(blocks,),
        in_specs=[
            pl.BlockSpec((params.shape[0], 8, LANES), lambda i: (0, i, 0)),
            pl.BlockSpec((8, LANES), lambda i: (0, 0)),
        ],
        out_specs=pl.BlockSpec((9, 8, LANES), lambda i: (0, i, 0)),
        out_shape=jax.ShapeDtypeStruct((9,) + params.shape[1:], F32),
        name="project",
    )(params, camera)


def lane_pick(rows, lanes):
    return jnp.take_along_axis(rows, lanes, axis=1, mode="promise_in_bounds")


def order_kernel(reps, request_ref, place_ref, out_ref):
    groups = request_ref.shape[0]
    place = place_ref[...].reshape(groups * reps, LANES)
    lanes = place & (LANES - 1)
    high = place >> 7
    result = jnp.zeros_like(place)
    for r in range(reps):
        table = jnp.broadcast_to(request_ref[:, r : r + 1, :], (groups, reps, LANES))
        picked = lane_pick(table.reshape(groups * reps, LANES), lanes)
        result = jnp.where(high == r, picked, result)
    out_ref[...] = result.reshape(groups, reps, LANES)


def invert_kernel(index_ref, out_ref):
    rows = index_ref.shape[0]
    high_iota = lax.broadcasted_iota(jnp.int32, (rows, 8 * LANES), 0)
    lane_iota = lax.broadcasted_iota(jnp.int32, (LANES, 8 * LANES), 0)
    column = lax.broadcasted_iota(jnp.int32, (1, 8 * LANES), 1)
    total = jnp.zeros((2 * rows, LANES), F32)
    for m in range(rows // 8):
        block = index_ref[8 * m : 8 * m + 8, :]
        flat = jnp.concatenate([block[s : s + 1] for s in range(8)], axis=1)
        hit = high_iota == (flat >> 7)
        row_value = (column // LANES + 8 * m).astype(F32)
        lane_value = (column % LANES).astype(F32)
        left = jnp.concatenate(
            [jnp.where(hit, row_value, 0.0), jnp.where(hit, lane_value, 0.0)], axis=0
        ).astype(BF16)
        right = jnp.where(lane_iota == (flat & (LANES - 1)), 1.0, 0.0).astype(BF16)
        total = total + lax.dot_general(
            left, right, (((1,), (1,)), ((), ())), preferred_element_type=F32
        )
    out_ref[...] = (total[:rows] * float(LANES) + total[rows:]).astype(jnp.int32)


def pick_block(load_row, index, source_rows):
    lanes = index & (LANES - 1)
    high = index >> 7

    def step(r, totals):
        hit = high == r
        return tuple(
            jnp.where(hit, lane_pick(jnp.broadcast_to(load_row(f, r), (8, LANES)), lanes), totals[f])
            for f in range(9)
        )

    start = tuple(jnp.zeros((8, LANES), F32) for _ in range(9))
    return lax.fori_loop(0, source_rows, step, start, unroll=8)


def gather_kernel(feature_ref, index_ref, out_ref):
    rows = feature_ref.shape[1]

    def block(m, carry):
        index = index_ref[pl.ds(pl.multiple_of(8 * m, 8), 8), :]
        picked = pick_block(lambda f, r: feature_ref[f, pl.ds(r, 1), :], index, rows)
        for f in range(9):
            out_ref[m, f] = picked[f]
        return carry

    lax.fori_loop(0, index_ref.shape[0] // 8, block, 0)


def ungather_kernel(grad_ref, index_ref, camera_ref, out_ref):
    rows = index_ref.shape[0]
    blocks = rows // 8

    def block(m, carry):
        index = index_ref[pl.ds(pl.multiple_of(8 * m, 8), 8), :]
        picked = pick_block(
            lambda f, r: grad_ref[r // 8, f, pl.ds(r % 8, 1), :], index, rows
        )
        for f in range(9):
            out_ref[f * blocks + m] = picked[f]
        return carry

    lax.fori_loop(0, blocks, block, 0)
    out_ref[9 * blocks] = camera_ref[...]


def backproject_kernel(views, blocks, params_ref, grad_ref, out_ref):
    m = pl.program_id(0)
    params = [params_ref[i] for i in range(11)]
    kept = [None] * 11
    for v in range(views):
        camera = unpack_camera(grad_ref[v, 9 * blocks])
        grads = [grad_ref[v, f * blocks + m] for f in range(9)]
        _, back = jax.vjp(lambda *p: geometry(list(p), camera), *params[0:10])
        shares = list(back(grads[0:5]))
        basis, back_dir = jax.vjp(lambda *c: directional(list(c), camera), *params[0:3])
        basis_grads = []
        for k in range(16):
            value = 0.0
            for h in range(3):
                at = 11 + 3 * k + h
                scale = sh_zero if k == 0 else basis[k - 1]
                share = scale * grads[6 + h]
                out_ref[at] = share if v == 0 else out_ref[at] + share
                if k:
                    value = value + params_ref[at] * grads[6 + h]
            if k:
                basis_grads.append(value)
        center_shares = back_dir(basis_grads)
        for i in range(3):
            shares[i] = shares[i] + center_shares[i]
        shares.append(grads[5] * jax.nn.sigmoid(-params[10]))
        kept = [s if t is None else t + s for s, t in zip(shares, kept)]
    for i in range(11):
        out_ref[i] = kept[i]


def backproject(params, grads):
    views, total = grads.shape[0], grads.shape[1]
    blocks = params.shape[1] // 8
    spec = pl.BlockSpec((params.shape[0], 8, LANES), lambda i: (0, i, 0))
    return pl.pallas_call(
        functools.partial(backproject_kernel, views, blocks),
        grid=(blocks,),
        in_specs=[
            spec,
            pl.BlockSpec((views, total, 8, LANES), lambda i: (0, 0, 0, 0)),
        ],
        out_specs=spec,
        out_shape=jax.ShapeDtypeStruct(params.shape, F32),
        name="backproject",
    )(params, grads)


def split_two(value):
    high = value.astype(BF16)
    return high, (value - high.astype(F32)).astype(BF16)


def split_three(value):
    high = value.astype(BF16).astype(F32)
    rest = value - high
    middle = rest.astype(BF16).astype(F32)
    return high, middle, rest - middle


def pixel_basis():
    pixel = np.arange(256)
    x = (pixel % 16) - 7.5
    y = (pixel // 16) - 7.5
    return np.stack([np.ones(256), x, y, x * x, x * y, y * y])


def spread_matrix():
    basis = pixel_basis()
    matrix = np.zeros((32, 640), np.float32)
    for s in range(3):
        matrix[9 * s : 9 * s + 6, :256] = basis
        for h in range(3):
            matrix[9 * s + 6 + h, 256 + 128 * h : 384 + 128 * h] = 1.0
    return jnp.asarray(matrix, BF16)


def moment_matrix():
    matrix = np.zeros((256, LANES), np.float32)
    matrix[:, 96:102] = pixel_basis().T
    return jnp.asarray(matrix, BF16)


def local_conic(feature_ref, m, center_u, center_v):
    shift_u = (feature_ref[m, 0] - center_u) * HALF
    shift_v = (feature_ref[m, 1] - center_v) * HALF
    scale = 1.0 / (HALF * HALF)
    return shift_u, shift_v, [feature_ref[m, 2 + i] * scale for i in range(3)]


def composite_kernel(
    feature_ref,
    meta_ref,
    pixel_grad_ref,
    spread_ref,
    moment_ref,
    image_ref,
    out_ref,
    coef_ref,
    alpha_ref,
    color_ref,
    weight_ref,
    shade_ref,
    reduce_ref,
    stage_a,
    stage_b,
    sums_ref,
    moments_ref,
):
    blocks = feature_ref.shape[0]
    rows = 8 * blocks
    center_u = meta_ref[0:1, :]
    center_v = meta_ref[1:2, :]
    lengths = meta_ref[2:3, :]
    lane = lax.broadcasted_iota(jnp.int32, (8, LANES), 1)
    sub = lax.broadcasted_iota(jnp.int32, (8, LANES), 0)

    for m in range(blocks):
        su, sv, (ca, cb, cc) = local_conic(feature_ref, m, center_u, center_v)
        place = ((8 * m + sub) * 8 + lane // 16).astype(F32)
        alive = place < lengths
        lin_u = ca * su + cb * sv
        lin_v = cb * su + cc * sv
        const = feature_ref[m, 5] - 0.5 * (lin_u * su + lin_v * sv)
        coefs = [const, lin_u, lin_v, -0.5 * ca, -cb, -0.5 * cc]
        dead = [-1.0e30, 0.0, 0.0, 0.0, 0.0, 0.0]
        coefs = [jnp.where(alive, c * LOG2E, d) for c, d in zip(coefs, dead)]
        coefs += [feature_ref[m, 6 + h] for h in range(3)]
        for i in range(9):
            for s, part in enumerate(split_three(coefs[i])):
                coef_ref[8 * m : 8 * m + 8, 9 * s + i, :] = part
        for i in range(27, 32):
            coef_ref[8 * m : 8 * m + 8, i, :] = jnp.zeros((8, LANES), F32)

    grads = pixel_grad_ref[...]
    high = grads.astype(BF16).astype(F32)
    stacked = jnp.concatenate([high, grads - high, jnp.zeros((32, 256), F32)], axis=0)
    by_pixel = jnp.transpose(stacked).astype(BF16)
    reduce_ref[0:256, :] = by_pixel
    reduce_ref[256:512, :] = by_pixel
    reduce_ref[512:768, :] = moment_ref[...]
    reduce_ref[768:1024, :] = moment_ref[...]

    def expand(i, carry):
        left = jnp.concatenate(
            [jnp.transpose(coef_ref[4 * i + s]) for s in range(4)], axis=0
        ).astype(BF16)
        spread = jnp.dot(left, spread_ref[...], preferred_element_type=F32)
        at = pl.ds(pl.multiple_of(512 * i, 512), 512)
        alpha_ref[at, :] = spread[:, 0:256]
        color_ref[at, :] = spread[:, 256:640]
        return carry

    lax.fori_loop(0, rows // 4, expand, 0)

    parts = [(g, b) for g in range(2) for b in range(2)]
    pixel_grads = {
        (g, b, h): pixel_grad_ref[16 * h + 8 * g : 16 * h + 8 * g + 8, 128 * b : 128 * b + 128]
        for g, b in parts
        for h in range(3)
    }

    def forward(q, carry):
        left, totals = list(carry[0]), list(carry[1])
        for kk in range(8):
            for g in range(2):
                at = pl.ds(pl.multiple_of(128 * q + 16 * kk + 8 * g, 8), 8)
                colors = [color_ref[at, 128 * h : 128 * h + 128] for h in range(3)]
                for b in range(2):
                    n = 2 * g + b
                    cols = slice(128 * b, 128 * b + 128)
                    alpha = jnp.exp2(alpha_ref[at, cols])
                    weight = alpha * left[n]
                    left[n] = left[n] - weight
                    shade = colors[0] * pixel_grads[g, b, 0]
                    shade = shade + colors[1] * pixel_grads[g, b, 1]
                    shade = shade + colors[2] * pixel_grads[g, b, 2]
                    for h in range(3):
                        totals[3 * n + h] = totals[3 * n + h] + weight * colors[h]
                    alpha_ref[at, cols] = alpha
                    weight_ref[at, cols] = weight
                    shade_ref[at, cols] = shade
        return tuple(left), tuple(totals)

    one = jnp.ones((8, LANES), F32)
    zero = jnp.zeros((8, LANES), F32)
    _, totals = lax.fori_loop(0, rows, forward, ((one,) * 4, (zero,) * 12))
    for n, (g, b) in enumerate(parts):
        for h in range(3):
            image_ref[8 * g : 8 * g + 8, h, 128 * b : 128 * b + 128] = totals[3 * n + h]

    def sweep(q, behind, stage):
        behind = list(behind)
        for kk in reversed(range(8)):
            for b in range(2):
                cols = slice(128 * b, 128 * b + 128)
                weights, slopes = [], []
                for g in range(2):
                    n = 2 * g + b
                    at = pl.ds(pl.multiple_of(128 * q + 16 * kk + 8 * g, 8), 8)
                    weight = weight_ref[at, cols]
                    gap = shade_ref[at, cols] - behind[n]
                    weights.append(weight)
                    slopes.append(weight * gap)
                    behind[n] = behind[n] + alpha_ref[at, cols] * gap
                split = split_two(jnp.concatenate(weights, axis=0))
                split += split_two(jnp.concatenate(slopes, axis=0))
                for i in range(4):
                    stage[16 * kk : 16 * kk + 16, 256 * i + 128 * b : 256 * i + 128 * b + 128] = split[i]
        return tuple(behind)

    def reduce_stage(q, stage):
        at = pl.ds(pl.multiple_of(128 * q, 128), 128)
        sums_ref[at, :] = jnp.dot(stage[...], reduce_ref[...], preferred_element_type=F32)

    stage_b[...] = jnp.zeros_like(stage_b)

    def backward(i, behind):
        q = rows - 1 - 2 * i
        reduce_stage(q + 1, stage_b)
        behind = sweep(q, behind, stage_a)
        reduce_stage(q, stage_a)
        return sweep(q - 1, behind, stage_b)

    lax.fori_loop(0, rows // 2, backward, (zero,) * 4)
    reduce_stage(0, stage_b)

    own = lax.broadcasted_iota(jnp.int32, (16, LANES), 0) == (
        lax.broadcasted_iota(jnp.int32, (16, LANES), 1) % 16
    )

    def collect(m, carry):
        for s in range(8):
            q = 8 * m + s
            at = pl.ds(pl.multiple_of(128 * q, 128), 128)
            turned = jnp.transpose(sums_ref[at, :])
            for i in range(6):
                moments_ref[i, s : s + 1, :] = turned[96 + i : 97 + i]
            for h in range(3):
                both = turned[16 * h : 16 * h + 16] + turned[48 + 16 * h : 64 + 16 * h]
                moments_ref[6 + h, s : s + 1, :] = jnp.sum(
                    jnp.where(own, both, 0.0), axis=0, keepdims=True
                )
        su, sv, (ca, cb, cc) = local_conic(feature_ref, m, center_u, center_v)
        m0, mx, my, mxx, mxy, myy = [moments_ref[i] for i in range(6)]
        scale = 1.0 / (HALF * HALF)
        dev_u = mx - su * m0
        dev_v = my - sv * m0
        out_ref[m, 0] = HALF * (ca * dev_u + cb * dev_v)
        out_ref[m, 1] = HALF * (cb * dev_u + cc * dev_v)
        out_ref[m, 2] = -0.5 * scale * (mxx - su * (mx + dev_u))
        out_ref[m, 3] = -scale * (mxy - su * my - sv * dev_u)
        out_ref[m, 4] = -0.5 * scale * (myy - sv * (my + dev_v))
        out_ref[m, 5] = m0
        for h in range(3):
            out_ref[m, 6 + h] = moments_ref[6 + h]
        return carry

    lax.fori_loop(0, blocks, collect, 0)


def composite(features, meta, pixel_grad, tiles):
    blocks = features.shape[0]
    count = blocks * 8 * LANES
    return pl.pallas_call(
        composite_kernel,
        in_specs=[VMEM] * 5,
        out_specs=[VMEM] * 2,
        out_shape=[
            jax.ShapeDtypeStruct((tiles, 3, 256), F32),
            jax.ShapeDtypeStruct((blocks, 9, 8, LANES), F32),
        ],
        scratch_shapes=[
            pltpu.VMEM((8 * blocks, 32, LANES), F32),
            pltpu.VMEM((count, 256), F32),
            pltpu.VMEM((count, 384), F32),
            pltpu.VMEM((count, 256), F32),
            pltpu.VMEM((count, 256), F32),
            pltpu.VMEM((1024, LANES), BF16),
            pltpu.VMEM((128, 1024), BF16),
            pltpu.VMEM((128, 1024), BF16),
            pltpu.VMEM((count + 128, LANES), F32),
            pltpu.VMEM((9, 8, LANES), F32),
        ],
        compiler_params=pltpu.CompilerParams(vmem_limit_bytes=56 * 1024 * 1024),
        name="composite",
    )(features, meta, pixel_grad, spread_matrix(), moment_matrix())


def to_blocks(sent):
    groups, width, reps, _ = sent.shape
    if reps == 8:
        return sent
    rows = sent.transpose(0, 2, 1, 3).reshape(groups * reps // 8, 8, width, LANES)
    return rows.transpose(0, 2, 1, 3)


def from_blocks(blocked, groups, reps):
    if reps == 8:
        return blocked
    width = blocked.shape[1]
    rows = blocked.transpose(0, 2, 1, 3).reshape(groups, reps, width, LANES)
    return rows.transpose(0, 2, 1, 3)


def simple_call(kernel, shape, dtype, name, *args):
    return pl.pallas_call(
        kernel,
        in_specs=[VMEM] * len(args),
        out_specs=VMEM,
        out_shape=jax.ShapeDtypeStruct(shape, dtype),
        name=name,
    )(*args)


def exchange(sent):
    return lax.all_to_all(sent, "space", split_axis=0, concat_axis=0, tiled=True)


def per_device(
    gaussians, camera_table, view_camera, tile_plan, requests, tile_lists, tile_lengths, pixel_grad
):
    groups, cap = requests.shape[2:]
    reps = cap // LANES
    tiles, span = tile_lists.shape[1:]
    slots = gaussians.shape[1]
    rows = slots // LANES
    blocks = rows // 8

    base = jnp.arange(groups, dtype=jnp.int32)[:, None] * cap
    place = tile_lists[0].T.reshape(groups, cap) - base
    wanted = simple_call(
        functools.partial(order_kernel, reps),
        (groups, reps, LANES),
        jnp.int32,
        "order",
        requests[0, 0].reshape(groups, reps, LANES),
        place.reshape(groups, reps, LANES),
    )
    incoming = exchange(wanted).reshape(groups * reps, LANES)

    chosen = (jnp.arange(camera_table.shape[0], dtype=jnp.int32) == view_camera[0]).astype(F32)
    camera = jnp.sum(camera_table * chosen[:, None], axis=0)
    camera = jnp.broadcast_to(camera[:, None], (8, LANES))
    params = gaussians.reshape(gaussians.shape[0], rows, LANES)
    features = project_all(params, camera)

    sent = simple_call(
        gather_kernel, (groups * reps // 8, 9, 8, LANES), F32, "gather", features, incoming
    )
    arrived = to_blocks(exchange(from_blocks(sent, groups, reps)))
    inverse = simple_call(invert_kernel, (rows, LANES), jnp.int32, "invert", incoming)

    plan = tile_plan[0]
    center_u = ((plan % 120 * 16 + 8).astype(F32) - 960.0) / HALF
    center_v = ((plan // 120 * 16 + 8).astype(F32) - 540.0) / HALF
    meta = jnp.stack([center_u, center_v, tile_lengths[0].astype(F32)])
    meta = jnp.tile(meta, (1, LANES // tiles))
    by_color = pixel_grad[0].transpose(1, 0, 2).reshape(3 * tiles, 256)
    image, row_grads = composite(arrived, meta, by_color, tiles)

    returned = to_blocks(exchange(from_blocks(row_grads, groups, reps)))
    packed = simple_call(
        ungather_kernel, (9 * blocks + 1, 8, LANES), F32, "ungather", returned, inverse, camera
    )
    every = lax.all_gather(packed, "view")
    total = backproject(params, every)
    return (image[None], total.reshape(gaussians.shape))


def solution(mesh):
    placed = (
        P(None, "space"),
        P(),
        P("view"),
        P("view", "space"),
        P("view", "space", None, None),
        P("view", "space", None),
        P("view", "space"),
        P("view", "space", None, None),
    )
    return jax.shard_map(
        per_device,
        mesh=mesh,
        in_specs=placed,
        out_specs=(P("view", "space", None, None), P(None, "space")),
        check_vma=False,
    )
```

time: 562 us -> 150 us (0.27); the launches traced: 554 us -> 149 us
  local copies, waits for them, and re-layouts: 154 us -> 14.8 us
  other arithmetic: 131 us -> 0.85 us
  matrix products: 71.9 us -> 0 us
  Pallas kernels: 0 us -> 71.7 us
  waiting for transfers between devices: 102 us -> 30.3 us
  blocking collectives: 51.8 us -> 0 us
  between operations: 30.8 us -> 14.8 us
  starting transfers between devices: 11.2 us -> 16.9 us
    scatter-add x2 -> x0, other arithmetic: 93.2 us -> none  [the longest x1 46.6 us: per_device(): local_grad = jnp.zeros_like(gaussians).at[:, incoming].add(returned)]
    dot_general x5 -> x0, matrix products: 71.9 us -> none  [the longest x2 40.3 us: composite(): before = jnp.einsum('tpk,kj->tpj', logs, triangle(span), precision=highest)]
    pallas_call x0 -> x7, Pallas kernels: none -> 71.7 us  [the longest x1 32.2 us: composite(): pl.pallas_call(composite_kernel, in_specs=[VMEM] * 5, out_specs=[VMEM] *...]
    psum x1 -> x0, waiting for transfers between devices: 70 us -> none  [per_device(): total = lax.psum(local_grad, 'view')]
    gather x4 -> x0, local copies, waits for them, and re-layouts: 65.7 us -> none  [the longest x2 32.9 us: composite(): jnp.take(features, entries.reshape(-1), axis=1)]
    all_to_all x1 -> x0, blocking collectives: 51.8 us -> none  [per_device(): lax.all_to_all(row_grad, 'space', split_axis=1, concat_axis=1, tiled=True)]
    another operation x3 -> x2, local copies, waits for them, and re-layouts: 38.4 us -> 0.66 us  [per_device(): meta = jnp.tile(meta, (1, LANES // tiles))]
    unnamed x255 -> x17, local copies, waits for them, and re-layouts: 39.7 us -> 11.1 us
  transfers between devices with their start and end apart: 3 -> 4, of which waited for: 3 -> 3; matrix products, arithmetic and copies ran while one was open for 4% -> 4% of each run, Pallas kernels for 0% -> 5%
where the time goes in v1:
time: 150 us; the launch traced here: 149 us
  Pallas kernels  71.7 us (48%)
  waiting for transfers between devices  30.3 us (20%)
  starting transfers between devices  16.9 us (11%)
  local copies, waits for them, and re-layouts  14.8 us (10%)
  between operations  14.8 us (10%)
    pallas_call x1, Pallas kernels, composite(): pl.pallas_call(composite_kernel, in_specs=[VMEM] * 5, out_specs=[VMEM] *...  32.2 us
    pallas_call x4, Pallas kernels, simple_call(): pl.pallas_call(kernel, in_specs=[VMEM] * len(args), out_specs=VMEM, out_s...  25.9 us
    all_to_all x3, starting transfers between devices, exchange(): lax.all_to_all(sent, 'space', split_axis=0, concat_axis=0, tiled=True)  16.9 us
    all_gather x1, waiting for transfers between devices, per_device(): every = lax.all_gather(packed, 'view')  15.3 us
    all_to_all x3, waiting for transfers between devices, exchange(): lax.all_to_all(sent, 'space', split_axis=0, concat_axis=0, tiled=True)  15 us
    unnamed x17, local copies, waits for them, and re-layouts  11.1 us
    pallas_call x1, Pallas kernels, backproject(): pl.pallas_call(functools.partial(backproject_kernel, views, blocks), grid...  8.05 us
    pallas_call x1, Pallas kernels, project_all(): pl.pallas_call(project_kernel, grid=(blocks,), in_specs=[pl.BlockSpec((pa...  5.49 us
  transfers between devices with their start and end apart: 4, of which 3 were waited for; matrix products, arithmetic and copies ran while one was open for 4% of the time, Pallas kernels for 5%

profile of v1, /device:TPU:0, one launch (start us, length us, event | category | flops | bytes accessed | tf_op | source)
XLA Modules:
  0.0 149.4 jit_solution(2715799867746573569)
XLA Ops:
  7.2 1.4 copy.22
  8.6 0.9 copy.16
  9.4 0.1 reshape.42
  9.6 0.7 broadcast_subtract_fusion.place_ref
  10.3 1.6 %order.1 = s32[8,8,128]{2,1,0:T(8,128)} custom-call(s32[8,8,128]{2,1,0:T(8,128)} %bitcast.32, s32[8,8,128]{2,1,0:T(8,128)} %broadcast_subtract_fusion.place_ref), custom_call_target="tpu_custom_call" | custom-call | tf_op jit(solution)/shard_map/order/pallas_call | solution.py:535
  11.9 7.3 %all-to-all-start = ((s32[8,8,128]{2,1,0:T(8,128)}), s32[8,8,128]{2,1,0:T(8,128)S(1)}, u32[]{:S(2)}, u32[]{:S(2)}) async-start(s32[8,8,128]{2,1,0:T(8,128)} %order.1), calls=%async_computation | async-start | bytes 65536 | tf_op jit(solution)/shard_map/all_to_all | solution.py:545
  19.8 2.0 %copy.18 = f32[8,8,64,128]{3,2,1,0:T(8,128)S(1)} copy(f32[8,8,64,128]{3,1,2,0:T(8,128)} %bitcast.27) | data formatting | bytes 4194304
  21.8 0.0 copy-start.3
  21.8 1.4 slice.params_ref
  23.2 0.0 copy-done.3
  23.2 0.0 copy-start.4
  23.2 0.0 copy-start.5
  23.2 0.1 multiply_reduce_fusion
  23.3 0.7 broadcast_in_dim.4.camera_ref
  24.0 5.5 %project.1.feature_ref = f32[9,64,128]{2,1,0:T(8,128)} custom-call(f32[59,64,128]{2,1,0:T(8,128)} %slice.params_ref, f32[8,128]{1,0:T(8,128)} %broadcast_in_dim.4.camera_ref), custom_call_target="tpu_custom_call" | custom-call | tf_op jit(solution)/shard_map/project/pallas_call | solution.py:132
  29.5 0.0 all-to-all-done
  29.5 0.0 copy-start.2
  29.5 0.6 copy-done.2
  30.1 11.0 %gather.1 = f32[8,9,8,128]{3,2,1,0:T(8,128)} custom-call(f32[9,64,128]{2,1,0:T(8,128)} %project.1.feature_ref, s32[64,128]{1,0:T(8,128)} %bitcast.30), custom_call_target="tpu_custom_call" | custom-call | tf_op jit(solution)/shard_map/gather/pallas_call | solution.py:535
  41.1 6.0 %all-to-all-start.1 = ((f32[8,9,8,128]{3,2,1,0:T(8,128)}), f32[8,9,8,128]{3,2,1,0:T(8,128)S(1)}, u32[]{:S(2)}, u32[]{:S(2)}) async-start(f32[8,9,8,128]{3,2,1,0:T(8,128)} %gather.1), calls=%async_computation.1 | async-start | bytes 589824 | tf_op jit(solution)/shard_map/all_to_all | solution.py:545
  47.1 0.0 copy-done.4
  47.2 0.0 copy-done.5
  47.2 0.7 tile.10.meta_ref
  47.9 8.3 %all-to-all-done.1.feature_ref = f32[8,9,8,128]{3,2,1,0:T(8,128)S(1)} async-done(((f32[8,9,8,128]{3,2,1,0:T(8,128)}), f32[8,9,8,128]{3,2,1,0:T(8,128)S(1)}, u32[]{:S(2)}, u32[]{:S(2)}) %all-to-all-start.1) | async-done | bytes 294944 | tf_op jit(solution)/shard_map/all_to_all | solution.py:545
  56.1 0.0 copy-start.1
  56.1 0.7 copy-done.1
  56.9 32.2 %composite.1 = (f32[16,3,256]{2,1,0:T(4,128)}, f32[8,9,8,128]{3,2,1,0:T(8,128)}) custom-call(f32[8,9,8,128]{3,2,1,0:T(8,128)} %copy-done.1, f32[3,128]{1,0:T(4,128)} %tile.10.meta_ref, f32[48,256]{1,0:T(8,128)} %bitcast.34, bf16[32,640]{1,0:T(8,128)(2,1)} %constant.41.clone.spread_ref, bf16[256,128]{1,0:T(8,128)(2,1)} %constant.42.clone.moment_ref), custom_call_target="tpu_custom_call" | custom-call | tf_op jit(solution)/shard_map/composite/pallas_call | solution.py:493
  89.0 3.6 %all-to-all-start.2 = ((f32[8,9,8,128]{3,2,1,0:T(8,128)}), f32[8,9,8,128]{3,2,1,0:T(8,128)S(1)}, u32[]{:S(2)}, u32[]{:S(2)}) async-start(f32[8,9,8,128]{3,2,1,0:T(8,128)} %get-tuple-element.5), calls=%async_computation.2 | async-start | bytes 589824 | tf_op jit(solution)/shard_map/all_to_all | solution.py:545
  92.7 0.0 all-gather.3.cloned.1.call-start
  92.7 2.2 %invert.1.index_ref = s32[64,128]{1,0:T(8,128)} custom-call(s32[64,128]{1,0:T(8,128)} %bitcast.31), custom_call_target="tpu_custom_call" | custom-call | tf_op jit(solution)/shard_map/invert/pallas_call | solution.py:535
  95.0 6.7 %all-to-all-done.2.grad_ref = f32[8,9,8,128]{3,2,1,0:T(8,128)S(1)} async-done(((f32[8,9,8,128]{3,2,1,0:T(8,128)}), f32[8,9,8,128]{3,2,1,0:T(8,128)S(1)}, u32[]{:S(2)}, u32[]{:S(2)}) %all-to-all-start.2) | async-done | bytes 294944 | tf_op jit(solution)/shard_map/all_to_all | solution.py:545
  101.7 0.0 copy-start
  101.7 0.7 copy-done
  102.4 11.0 %ungather.1 = f32[73,8,128]{2,1,0:T(8,128)} custom-call(f32[8,9,8,128]{3,2,1,0:T(8,128)} %copy-done, s32[64,128]{1,0:T(8,128)} %invert.1.index_ref, f32[8,128]{1,0:T(8,128)} %broadcast_in_dim.4.camera_ref), custom_call_target="tpu_custom_call" | custom-call | tf_op jit(solution)/shard_map/ungather/pallas_call | solution.py:535
  113.4 0.0 all-gather.3.cloned.1.call-update
  113.5 1.5 copy.17
  114.9 15.3 %all-gather.3.cloned.1.call-done = f32[292,8,128]{2,1,0:T(8,128)} async-done(((f32[73,8,128]{2,1,0:T(8,128)}), f32[292,8,128]{2,1,0:T(8,128)}) %all-gather.3.cloned.1.call-update) | async-done | bytes 1196048 | tf_op jit(solution)/shard_map/all_gather | solution.py:594
  130.2 8.1 %backproject.1 = f32[59,64,128]{2,1,0:T(8,128)} custom-call(f32[59,64,128]{2,1,0:T(8,128)} %slice.params_ref, f32[4,73,8,128]{3,2,1,0:T(8,128)} %bitcast.29), custom_call_target="tpu_custom_call" | custom-call | tf_op jit(solution)/shard_map/backproject/pallas_call | solution.py:264
  138.3 1.7 %pad.3 = f32[64,64,128]{2,1,0:T(8,128)S(1)} pad(f32[59,64,128]{2,1,0:T(8,128)} %backproject.1, f32[]{:T(128)} %constant.30.clone.1), padding=0_5x0_0x0_0 | pad | bytes 4030468
  140.0 2.5 %copy.20 = f32[8,8,64,128]{3,1,2,0:T(8,128)} copy(f32[8,8,64,128]{3,2,1,0:T(8,128)S(1)} %bitcast.25) | data formatting | bytes 4194304
  (6 shorter events, 0.0 us)
Async XLA Ops:
  11.9 17.6 %all-to-all-start = ((s32[8,8,128]{2,1,0:T(8,128)}), s32[8,8,128]{2,1,0:T(8,128)S(1)}, u32[]{:S(2)}, u32[]{:S(2)}) async-start(s32[8,8,128]{2,1,0:T(8,128)} %order.1), calls=%async_computation | async-start | bytes 65536 | tf_op jit(solution)/shard_map/all_to_all | solution.py:545
  21.8 1.4 copy-start.3
  23.2 23.9 %copy-start.4 = (s32[1,16]{1,0:T(1,128)S(1)}, s32[1,16]{1,0:T(1,128)}, u32[]{:S(2)}) copy-start(s32[1,16]{1,0:T(1,128)} %param.16) | copy-start | bytes 196
  23.2 23.9 %copy-start.5 = (s32[1,16]{1,0:T(1,128)S(1)}, s32[1,16]{1,0:T(1,128)}, u32[]{:S(2)}) copy-start(s32[1,16]{1,0:T(1,128)} %param.13) | copy-start | bytes 196
  29.5 0.6 copy-start.2
  41.1 15.0 %all-to-all-start.1 = ((f32[8,9,8,128]{3,2,1,0:T(8,128)}), f32[8,9,8,128]{3,2,1,0:T(8,128)S(1)}, u32[]{:S(2)}, u32[]{:S(2)}) async-start(f32[8,9,8,128]{3,2,1,0:T(8,128)} %gather.1), calls=%async_computation.1 | async-start | bytes 589824 | tf_op jit(solution)/shard_map/all_to_all | solution.py:545
  56.1 0.7 copy-start.1
  89.0 12.6 %all-to-all-start.2 = ((f32[8,9,8,128]{3,2,1,0:T(8,128)}), f32[8,9,8,128]{3,2,1,0:T(8,128)S(1)}, u32[]{:S(2)}, u32[]{:S(2)}) async-start(f32[8,9,8,128]{3,2,1,0:T(8,128)} %get-tuple-element.5), calls=%async_computation.2 | async-start | bytes 589824 | tf_op jit(solution)/shard_map/all_to_all | solution.py:545
  92.7 37.5 %all-gather.3.cloned.1.call-start = ((), (), s32[]{:S(2)}) async-start(), calls=%async_computation.3 | async-start | bytes 1495040 | tf_op jit(solution)/shard_map/all_gather | solution.py:594
  101.7 0.7 copy-start
Sparse Core Ops, SparseCore 0:
  113.6 16.5 all-gather.2

commit v2 on v1

--- a/solution.py
+++ b/solution.py
@@ -111,18 +111,22 @@
     return (quat_matrix(*full[0:4]), full[4:7], full[7])
 
 
-def project_kernel(params_ref, camera_ref, out_ref):
-    camera = unpack_camera(camera_ref[...])
-    params = [params_ref[i] for i in range(11)]
+def project_block(load, camera):
+    params = [load(i) for i in range(11)]
     feats = geometry(params, camera)
     logit = params[10]
     feats.append(jnp.minimum(logit, 0.0) - jnp.log1p(jnp.exp(-jnp.abs(logit))))
     basis = directional(params[0:3], camera)
     for h in range(3):
-        total = 0.5 + sh_zero * params_ref[11 + h]
+        total = 0.5 + sh_zero * load(11 + h)
         for k in range(1, 16):
-            total = total + basis[k - 1] * params_ref[11 + 3 * k + h]
+            total = total + basis[k - 1] * load(11 + 3 * k + h)
         feats.append(total)
+    return feats
+
+
+def project_kernel(params_ref, camera_ref, out_ref):
+    feats = project_block(lambda i: params_ref[i], unpack_camera(camera_ref[...]))
     for i in range(9):
         out_ref[i] = feats[i]
 
@@ -146,31 +150,34 @@
     return jnp.take_along_axis(rows, lanes, axis=1, mode="promise_in_bounds")
 
 
-def order_kernel(reps, request_ref, place_ref, out_ref):
-    groups = request_ref.shape[0]
-    place = place_ref[...].reshape(groups * reps, LANES)
+def order_rows(requests, place):
+    groups, reps = place.shape[:2]
+    place = place.reshape(groups * reps, LANES)
     lanes = place & (LANES - 1)
     high = place >> 7
     result = jnp.zeros_like(place)
     for r in range(reps):
-        table = jnp.broadcast_to(request_ref[:, r : r + 1, :], (groups, reps, LANES))
+        table = jnp.broadcast_to(requests[:, r : r + 1, :], (groups, reps, LANES))
         picked = lane_pick(table.reshape(groups * reps, LANES), lanes)
         result = jnp.where(high == r, picked, result)
-    out_ref[...] = result.reshape(groups, reps, LANES)
-
-
-def invert_kernel(index_ref, out_ref):
-    rows = index_ref.shape[0]
+    return result.reshape(groups, reps, LANES)
+
+
+def order_kernel(request_ref, place_ref, out_ref):
+    out_ref[...] = order_rows(request_ref[...], place_ref[...])
+
+
+def invert_rows(blocks):
+    rows = 8 * len(blocks)
     high_iota = lax.broadcasted_iota(jnp.int32, (rows, 8 * LANES), 0)
     lane_iota = lax.broadcasted_iota(jnp.int32, (LANES, 8 * LANES), 0)
     column = lax.broadcasted_iota(jnp.int32, (1, 8 * LANES), 1)
     total = jnp.zeros((2 * rows, LANES), F32)
-    for m in range(rows // 8):
-        block = index_ref[8 * m : 8 * m + 8, :]
+    for m, block in enumerate(blocks):
         flat = jnp.concatenate([block[s : s + 1] for s in range(8)], axis=1)
         hit = high_iota == (flat >> 7)
-        row_value = (column // LANES + 8 * m).astype(F32)
-        lane_value = (column % LANES).astype(F32)
+        row_value = ((column >> 7) + 8 * m).astype(F32)
+        lane_value = (column & (LANES - 1)).astype(F32)
         left = jnp.concatenate(
             [jnp.where(hit, row_value, 0.0), jnp.where(hit, lane_value, 0.0)], axis=0
         ).astype(BF16)
@@ -178,7 +185,12 @@
         total = total + lax.dot_general(
             left, right, (((1,), (1,)), ((), ())), preferred_element_type=F32
         )
-    out_ref[...] = (total[:rows] * float(LANES) + total[rows:]).astype(jnp.int32)
+    return (total[:rows] * float(LANES) + total[rows:]).astype(jnp.int32)
+
+
+def invert_kernel(index_ref, out_ref):
+    rows = index_ref.shape[0]
+    out_ref[...] = invert_rows([index_ref[8 * m : 8 * m + 8, :] for m in range(rows // 8)])
 
 
 def pick_block(load_row, index, source_rows):
@@ -226,15 +238,12 @@
     out_ref[9 * blocks] = camera_ref[...]
 
 
-def backproject_kernel(views, blocks, params_ref, grad_ref, out_ref):
-    m = pl.program_id(0)
-    params = [params_ref[i] for i in range(11)]
+def backproject_block(load, cameras, grads, load_out, store_out):
+    params = [load(i) for i in range(11)]
     kept = [None] * 11
-    for v in range(views):
-        camera = unpack_camera(grad_ref[v, 9 * blocks])
-        grads = [grad_ref[v, f * blocks + m] for f in range(9)]
+    for v, camera in enumerate(cameras):
         _, back = jax.vjp(lambda *p: geometry(list(p), camera), *params[0:10])
-        shares = list(back(grads[0:5]))
+        shares = list(back(grads[v][0:5]))
         basis, back_dir = jax.vjp(lambda *c: directional(list(c), camera), *params[0:3])
         basis_grads = []
         for k in range(16):
@@ -242,19 +251,275 @@
             for h in range(3):
                 at = 11 + 3 * k + h
                 scale = sh_zero if k == 0 else basis[k - 1]
-                share = scale * grads[6 + h]
-                out_ref[at] = share if v == 0 else out_ref[at] + share
+                share = scale * grads[v][6 + h]
+                store_out(at, share if v == 0 else load_out(at) + share)
                 if k:
-                    value = value + params_ref[at] * grads[6 + h]
+                    value = value + load(at) * grads[v][6 + h]
             if k:
                 basis_grads.append(value)
         center_shares = back_dir(basis_grads)
         for i in range(3):
             shares[i] = shares[i] + center_shares[i]
-        shares.append(grads[5] * jax.nn.sigmoid(-params[10]))
+        shares.append(grads[v][5] * jax.nn.sigmoid(-params[10]))
         kept = [s if t is None else t + s for s, t in zip(shares, kept)]
     for i in range(11):
-        out_ref[i] = kept[i]
+        store_out(i, kept[i])
+
+
+def backproject_kernel(views, blocks, params_ref, grad_ref, out_ref):
+    m = pl.program_id(0)
+
+    def store(i, value):
+        out_ref[i] = value
+
+    backproject_block(
+        lambda i: params_ref[i],
+        [unpack_camera(grad_ref[v, 9 * blocks]) for v in range(views)],
+        [[grad_ref[v, f * blocks + m] for f in range(9)] for v in range(views)],
+        lambda i: out_ref[i],
+        store,
+    )
+
+
+def remote(src, dst, send, recv, device):
+    return pltpu.make_async_remote_copy(
+        src_ref=src,
+        dst_ref=dst,
+        send_sem=send,
+        recv_sem=recv,
+        device_id=device,
+        device_id_type=pl.DeviceIdType.MESH,
+    )
+
+
+def request_kernel(
+    groups,
+    request_ref,
+    place_ref,
+    params_ref,
+    camera_ref,
+    arrived_ref,
+    inverse_ref,
+    wanted,
+    incoming,
+    features,
+    outbox,
+    ask_send,
+    ask_recv,
+    row_send,
+    row_recv,
+):
+    me = lax.axis_index("space")
+    view = lax.axis_index("view")
+    rows = features.shape[1]
+
+    def peer(d):
+        return lax.rem(me + (d + groups), groups)
+
+    barrier = pltpu.get_barrier_semaphore()
+    for d in range(1, groups):
+        pl.semaphore_signal(
+            barrier, inc=1, device_id=(peer(d), view), device_id_type=pl.DeviceIdType.MESH
+        )
+    wanted[...] = order_rows(request_ref[...], place_ref[...])
+    pl.semaphore_wait(barrier, groups - 1)
+
+    asks = []
+    for d in range(1, groups):
+        to = peer(d)
+        ask = remote(
+            wanted.at[to], incoming.at[me], ask_send.at[d], ask_recv.at[d], (to, view)
+        )
+        ask.start()
+        asks.append(ask)
+    incoming[me] = wanted[me]
+
+    camera = unpack_camera(camera_ref[...])
+
+    def project(m, carry):
+        at = pl.ds(pl.multiple_of(8 * m, 8), 8)
+        feats = project_block(lambda i: params_ref[i, at, :], camera)
+        for i in range(9):
+            features[i, at, :] = feats[i]
+        return carry
+
+    lax.fori_loop(0, rows // 8, project, 0)
+
+    answers = []
+    for d in range(groups):
+        if d:
+            asks[d - 1].wait_recv()
+        to = peer(-d)
+        picked = pick_block(lambda f, r: features[f, pl.ds(r, 1), :], incoming[to], rows)
+        box = outbox.at[d] if d else arrived_ref.at[me]
+        for f in range(9):
+            box[f] = picked[f]
+        if d:
+            answer = remote(
+                outbox.at[d], arrived_ref.at[me], row_send.at[d], row_recv.at[d], (to, view)
+            )
+            answer.start()
+            answers.append(answer)
+    inverse_ref[...] = invert_rows([incoming[s] for s in range(groups)])
+    for ask in asks:
+        ask.wait_send()
+    for answer in answers:
+        answer.wait()
+
+
+def request_rows(requests, place, params, camera):
+    groups = requests.shape[0]
+    rows = params.shape[1]
+    return pl.pallas_call(
+        functools.partial(request_kernel, groups),
+        in_specs=[VMEM] * 4,
+        out_specs=[VMEM] * 2,
+        out_shape=[
+            jax.ShapeDtypeStruct((groups, 9, 8, LANES), F32),
+            jax.ShapeDtypeStruct((rows, LANES), jnp.int32),
+        ],
+        scratch_shapes=[
+            pltpu.VMEM((groups, 8, LANES), jnp.int32),
+            pltpu.VMEM((groups, 8, LANES), jnp.int32),
+            pltpu.VMEM((9, rows, LANES), F32),
+            pltpu.VMEM((groups, 9, 8, LANES), F32),
+        ]
+        + [pltpu.SemaphoreType.DMA((groups,))] * 4,
+        compiler_params=pltpu.CompilerParams(
+            collective_id=0, has_side_effects=True, vmem_limit_bytes=32 * 1024 * 1024
+        ),
+        name="request",
+    )(requests, place, params, camera)
+
+
+def return_kernel(
+    groups,
+    grad_ref,
+    index_ref,
+    camera_ref,
+    params_ref,
+    out_ref,
+    landed,
+    every,
+    cameras,
+    row_send,
+    row_recv,
+    cam_send,
+    cam_recv,
+    view_send,
+    view_recv,
+):
+    me = lax.axis_index("space")
+    view = lax.axis_index("view")
+    core = lax.rem(view, 2)
+    beside = view + 1 - 2 * core
+    across = lax.rem(view + 2, 4)
+    diagonal = lax.rem(beside + 2, 4)
+    rows = index_ref.shape[0]
+    blocks = rows // 8
+
+    def peer(d):
+        return lax.rem(me + (d + groups), groups)
+
+    barrier = pltpu.get_barrier_semaphore()
+    for device in [(peer(d), view) for d in range(1, groups)] + [
+        (me, v) for v in (beside, across, diagonal)
+    ]:
+        pl.semaphore_signal(
+            barrier, inc=1, device_id=device, device_id_type=pl.DeviceIdType.MESH
+        )
+    pl.semaphore_wait(barrier, groups + 2)
+
+    moves = []
+    for d in range(1, groups):
+        to = peer(d)
+        move = remote(
+            grad_ref.at[to], landed.at[me], row_send.at[d], row_recv.at[d], (to, view)
+        )
+        move.start()
+        moves.append(move)
+    cameras[view] = camera_ref[...]
+    for i, v in enumerate((beside, across, diagonal)):
+        move = remote(
+            cameras.at[view], cameras.at[view], cam_send.at[i], cam_recv.at[i], (me, v)
+        )
+        move.start()
+        moves.append(move)
+    landed[me] = grad_ref[me]
+    for move in moves:
+        move.wait_recv()
+
+    def ship(kind, owner, m, v):
+        block = every.at[owner, m]
+        return remote(block, block, view_send.at[kind, m], view_recv.at[kind, m], (me, v))
+
+    def forward(m):
+        ship(1, view, m, across).wait_recv()
+        ship(2, across, m, beside).start()
+
+    for m in range(blocks):
+        picked = pick_block(
+            lambda f, r: landed[r // 8, f, pl.ds(r % 8, 1), :], index_ref[8 * m : 8 * m + 8, :], rows
+        )
+        for f in range(9):
+            every[view, m, f] = picked[f]
+        ship(0, view, m, beside).start()
+        ship(1, view, m, across).start()
+        if m >= 2:
+            forward(m - 2)
+    for m in range(blocks - 2, blocks):
+        forward(m)
+
+    def finish(m, carry):
+        ship(0, view, m, beside).wait_recv()
+        ship(2, across, m, beside).wait_recv()
+        at = pl.ds(pl.multiple_of(8 * m, 8), 8)
+
+        def store(i, value):
+            out_ref[i, at, :] = value
+
+        backproject_block(
+            lambda i: params_ref[i, at, :],
+            [unpack_camera(cameras[v]) for v in range(4)],
+            [[every[v, m, f] for f in range(9)] for v in range(4)],
+            lambda i: out_ref[i, at, :],
+            store,
+        )
+        return carry
+
+    lax.fori_loop(0, blocks, finish, 0)
+    for move in moves:
+        move.wait_send()
+    for m in range(blocks):
+        ship(0, view, m, beside).wait_send()
+        ship(1, view, m, across).wait_send()
+        ship(2, across, m, beside).wait_send()
+
+
+def return_rows(grads, inverse, camera, params):
+    groups = grads.shape[0]
+    rows = params.shape[1]
+    return pl.pallas_call(
+        functools.partial(return_kernel, groups),
+        in_specs=[VMEM] * 4,
+        out_specs=VMEM,
+        out_shape=jax.ShapeDtypeStruct(params.shape, F32),
+        scratch_shapes=[
+            pltpu.VMEM((groups, 9, 8, LANES), F32),
+            pltpu.VMEM((4, rows // 8, 9, 8, LANES), F32),
+            pltpu.VMEM((4, 8, LANES), F32),
+            pltpu.SemaphoreType.DMA((groups,)),
+            pltpu.SemaphoreType.DMA((groups,)),
+            pltpu.SemaphoreType.DMA((3,)),
+            pltpu.SemaphoreType.DMA((3,)),
+            pltpu.SemaphoreType.DMA((3, rows // 8)),
+            pltpu.SemaphoreType.DMA((3, rows // 8)),
+        ],
+        compiler_params=pltpu.CompilerParams(
+            collective_id=1, has_side_effects=True, vmem_limit_bytes=32 * 1024 * 1024
+        ),
+        name="return",
+    )(grads, inverse, camera, params)
 
 
 def backproject(params, grads):
@@ -546,7 +811,7 @@
 
 
 def per_device(
-    gaussians, camera_table, view_camera, tile_plan, requests, tile_lists, tile_lengths, pixel_grad
+    views, gaussians, camera_table, view_camera, tile_plan, requests, tile_lists, tile_lengths, pixel_grad
 ):
     groups, cap = requests.shape[2:]
     reps = cap // LANES
@@ -555,29 +820,26 @@
     rows = slots // LANES
     blocks = rows // 8
 
-    base = jnp.arange(groups, dtype=jnp.int32)[:, None] * cap
-    place = tile_lists[0].T.reshape(groups, cap) - base
-    wanted = simple_call(
-        functools.partial(order_kernel, reps),
-        (groups, reps, LANES),
-        jnp.int32,
-        "order",
-        requests[0, 0].reshape(groups, reps, LANES),
-        place.reshape(groups, reps, LANES),
-    )
-    incoming = exchange(wanted).reshape(groups * reps, LANES)
-
     chosen = (jnp.arange(camera_table.shape[0], dtype=jnp.int32) == view_camera[0]).astype(F32)
     camera = jnp.sum(camera_table * chosen[:, None], axis=0)
     camera = jnp.broadcast_to(camera[:, None], (8, LANES))
     params = gaussians.reshape(gaussians.shape[0], rows, LANES)
-    features = project_all(params, camera)
-
-    sent = simple_call(
-        gather_kernel, (groups * reps // 8, 9, 8, LANES), F32, "gather", features, incoming
-    )
-    arrived = to_blocks(exchange(from_blocks(sent, groups, reps)))
-    inverse = simple_call(invert_kernel, (rows, LANES), jnp.int32, "invert", incoming)
+
+    base = jnp.arange(groups, dtype=jnp.int32)[:, None] * cap
+    place = (tile_lists[0].T.reshape(groups, cap) - base).reshape(groups, reps, LANES)
+    asked = requests[0, 0].reshape(groups, reps, LANES)
+    fused = reps == 8 and rows == 8 * groups and views == 4
+    if fused:
+        arrived, inverse = request_rows(asked, place, params, camera)
+    else:
+        wanted = simple_call(order_kernel, place.shape, jnp.int32, "order", asked, place)
+        incoming = exchange(wanted).reshape(groups * reps, LANES)
+        features = project_all(params, camera)
+        sent = simple_call(
+            gather_kernel, (groups * reps // 8, 9, 8, LANES), F32, "gather", features, incoming
+        )
+        arrived = to_blocks(exchange(from_blocks(sent, groups, reps)))
+        inverse = simple_call(invert_kernel, (rows, LANES), jnp.int32, "invert", incoming)
 
     plan = tile_plan[0]
     center_u = ((plan % 120 * 16 + 8).astype(F32) - 960.0) / HALF
@@ -587,12 +849,14 @@
     by_color = pixel_grad[0].transpose(1, 0, 2).reshape(3 * tiles, 256)
     image, row_grads = composite(arrived, meta, by_color, tiles)
 
-    returned = to_blocks(exchange(from_blocks(row_grads, groups, reps)))
-    packed = simple_call(
-        ungather_kernel, (9 * blocks + 1, 8, LANES), F32, "ungather", returned, inverse, camera
-    )
-    every = lax.all_gather(packed, "view")
-    total = backproject(params, every)
+    if fused:
+        total = return_rows(row_grads, inverse, camera, params)
+    else:
+        returned = to_blocks(exchange(from_blocks(row_grads, groups, reps)))
+        packed = simple_call(
+            ungather_kernel, (9 * blocks + 1, 8, LANES), F32, "ungather", returned, inverse, camera
+        )
+        total = backproject(params, lax.all_gather(packed, "view"))
     return (image[None], total.reshape(gaussians.shape))
 
 
@@ -608,7 +872,7 @@
         P("view", "space", None, None),
     )
     return jax.shard_map(
-        per_device,
+        functools.partial(per_device, mesh.shape["view"]),
         mesh=mesh,
         in_specs=placed,
         out_specs=(P("view", "space", None, None), P(None, "space")),

time: 150 us -> 92.2 us (0.61)
  waiting for transfers between devices: 30.3 us -> 0 us
  starting transfers between devices: 16.9 us -> 0 us
  between operations: 14.8 us -> 1.41 us
  Pallas kernels: 71.7 us -> 79.6 us
  local copies, waits for them, and re-layouts: 14.8 us -> 10.6 us
    all_to_all x3 -> x0, starting transfers between devices: 16.9 us -> none  [exchange(): lax.all_to_all(sent, 'space', split_axis=0, concat_axis=0, tiled=True)]
    all_gather x1 -> x0, waiting for transfers between devices: 15.3 us -> none  [per_device(): every = lax.all_gather(packed, 'view')]
    all_to_all x3 -> x0, waiting for transfers between devices: 15 us -> none  [exchange(): lax.all_to_all(sent, 'space', split_axis=0, concat_axis=0, tiled=True)]
    pallas_call x6 -> x2, Pallas kernels: 39.5 us -> 47.4 us  [the longest x1 27.4 us: return_rows(): pl.pallas_call(functools.partial(return_kernel, groups), in_specs=[VMEM]...]
    unnamed x17 -> x15, local copies, waits for them, and re-layouts: 11.1 us -> 8.61 us
  transfers between devices with their start and end apart: 4 -> 0, of which waited for: 3 -> 0; matrix products, arithmetic and copies ran while one was open for 4% -> 0% of each run, Pallas kernels for 5% -> 0%
where the time goes in v2:
time: 92.2 us; the launch traced here: 91.8 us
  Pallas kernels  79.6 us (86%)
  local copies, waits for them, and re-layouts  10.6 us (11%)
  between operations  1.41 us (2%)
    pallas_call x1, Pallas kernels, composite(): pl.pallas_call(composite_kernel, in_specs=[VMEM] * 5, out_specs=[VMEM] *...  32.2 us
    pallas_call x1, Pallas kernels, return_rows(): pl.pallas_call(functools.partial(return_kernel, groups), in_specs=[VMEM]...  27.4 us
    pallas_call x1, Pallas kernels, request_rows(): pl.pallas_call(functools.partial(request_kernel, groups), in_specs=[VMEM]...  20 us
    unnamed x15, local copies, waits for them, and re-layouts  8.61 us

profile of v2, /device:TPU:0, one launch (start us, length us, event | category | flops | bytes accessed | tf_op | source)
XLA Modules:
  0.0 91.8 jit_solution(9034045437019638118)
XLA Ops:
  0.6 0.8 copy.20
  1.4 0.9 copy.14
  2.3 0.1 reshape.38
  2.4 0.1 broadcast_subtract_fusion.place_ref
  2.5 2.0 %copy.17 = f32[8,8,64,128]{3,2,1,0:T(8,128)S(1)} copy(f32[8,8,64,128]{3,1,2,0:T(8,128)} %bitcast.26) | data formatting | bytes 4194304
  4.5 0.0 copy-start.2
  4.5 0.0 copy-start.3
  4.5 0.0 copy-start.4
  4.5 0.2 slice.params_ref
  5.4 0.0 copy-done.2
  5.4 0.1 multiply_reduce_fusion
  5.5 0.1 broadcast_in_dim.4.camera_ref
  5.6 20.0 %request.1 = (f32[8,9,8,128]{3,2,1,0:T(8,128)S(1)}, s32[64,128]{1,0:T(8,128)S(1)}) custom-call(s32[8,8,128]{2,1,0:T(8,128)S(1)} %bitcast.23, s32[8,8,128]{2,1,0:T(8,128)S(1)} %broadcast_subtract_fusion.place_ref, f32[59,64,128]{2,1,0:T(8,128)S(1)} %slice.params_ref, f32[8,128]{1,0:T(8,128)S(1)} %broadcast_in_dim.4.camera_ref), custom_call_target="tpu_custom_call" | custom-call | tf_op jit(solution)/shard_map/request/pallas_call | solution.py:373
  25.6 0.0 copy-start.1
  25.7 0.7 copy-done.1
  26.4 0.0 copy-done.3
  26.4 0.0 copy-done.4
  26.4 0.7 tile.10.meta_ref
  27.1 32.2 %composite.1 = (f32[16,3,256]{2,1,0:T(4,128)}, f32[8,9,8,128]{3,2,1,0:T(8,128)}) custom-call(f32[8,9,8,128]{3,2,1,0:T(8,128)} %copy-done.1, f32[3,128]{1,0:T(4,128)} %tile.10.meta_ref, f32[48,256]{1,0:T(8,128)} %bitcast.29, bf16[32,640]{1,0:T(8,128)(2,1)} %constant.41.clone.spread_ref, bf16[256,128]{1,0:T(8,128)(2,1)} %constant.42.clone.moment_ref), custom_call_target="tpu_custom_call" | custom-call | tf_op jit(solution)/shard_map/composite/pallas_call | solution.py:758
  59.3 1.5 %copy.15 = f32[1,16,3,256]{3,1,2,0:T(8,128)} copy(f32[1,16,3,256]{3,2,1,0:T(4,128)} %bitcast.28) | data formatting | bytes 98304
  60.7 0.0 copy-start
  60.7 1.0 %copy-done = f32[8,9,8,128]{3,2,1,0:T(8,128)S(1)} copy-done((f32[8,9,8,128]{3,2,1,0:T(8,128)S(1)}, f32[8,9,8,128]{3,2,1,0:T(8,128)}, u32[]{:S(2)}) %copy-start) | copy-done | bytes 294936
  61.7 27.4 %return.1 = f32[59,64,128]{2,1,0:T(8,128)S(1)} custom-call(f32[8,9,8,128]{3,2,1,0:T(8,128)S(1)} %copy-done, s32[64,128]{1,0:T(8,128)S(1)} %get-tuple-element.9.index_ref, f32[8,128]{1,0:T(8,128)S(1)} %broadcast_in_dim.4.camera_ref, f32[59,64,128]{2,1,0:T(8,128)S(1)} %slice.params_ref), custom_call_target="tpu_custom_call" | custom-call | tf_op jit(solution)/shard_map/return/pallas_call | solution.py:502
  89.1 0.2 pad.3
  89.3 2.5 %copy.18 = f32[8,8,64,128]{3,1,2,0:T(8,128)} copy(f32[8,8,64,128]{3,2,1,0:T(8,128)S(1)} %bitcast.24) | data formatting | bytes 4194304
  (6 shorter events, 0.0 us)
Async XLA Ops:
  4.5 0.9 %copy-start.2 = (f32[16,8]{0,1:T(8,128)S(1)}, f32[16,8]{0,1:T(8,128)}, u32[]{:S(2)}) copy-start(f32[16,8]{0,1:T(8,128)} %param.11) | copy-start | bytes 1540
  4.5 21.9 %copy-start.3 = (s32[1,16]{1,0:T(1,128)S(1)}, s32[1,16]{1,0:T(1,128)}, u32[]{:S(2)}) copy-start(s32[1,16]{1,0:T(1,128)} %param.16) | copy-start | bytes 196
  4.5 21.9 %copy-start.4 = (s32[1,16]{1,0:T(1,128)S(1)}, s32[1,16]{1,0:T(1,128)}, u32[]{:S(2)}) copy-start(s32[1,16]{1,0:T(1,128)} %param.13) | copy-start | bytes 196
  25.6 0.7 copy-start.1
  60.7 1.0 %copy-start = (f32[8,9,8,128]{3,2,1,0:T(8,128)S(1)}, f32[8,9,8,128]{3,2,1,0:T(8,128)}, u32[]{:S(2)}) copy-start(f32[8,9,8,128]{3,2,1,0:T(8,128)} %get-tuple-element.8.grad_ref) | copy-start | bytes 884740

commit v3 on v2

--- a/solution.py
+++ b/solution.py
@@ -69,27 +69,29 @@
     ]
 
 
-def geometry(params, camera):
-    center = params[0:3]
-    scales = [jnp.exp(params[3]), jnp.exp(params[4]), jnp.exp(params[5])]
-    own_rot = quat_matrix(*params[6:10])
+def shape_axes(*params):
+    scales = [jnp.exp(params[0]), jnp.exp(params[1]), jnp.exp(params[2])]
+    own_rot = quat_matrix(*params[3:7])
+    return [own_rot[i][k] * scales[k] for i in range(3) for k in range(3)]
+
+
+def screen_conic(center, shaped, camera):
     view_rot, offset_cam, focal_len = camera
     in_camera = [
         sum((view_rot[i][j] * center[j] for j in range(3))) + offset_cam[i] for i in range(3)
     ]
-    shaped = [[own_rot[i][k] * scales[k] for k in range(3)] for i in range(3)]
     turned = [
-        [sum((view_rot[i][j] * shaped[j][k] for j in range(3))) for k in range(3)] for i in range(3)
+        [sum((view_rot[i][j] * shaped[3 * j + k] for j in range(3))) for k in range(3)]
+        for i in range(3)
     ]
     inv_depth = 1.0 / in_camera[2]
-    screen_u = focal_len * in_camera[0] * inv_depth
-    screen_v = focal_len * in_camera[1] * inv_depth
-    jac_u = [
-        focal_len * inv_depth * turned[0][k] - screen_u * inv_depth * turned[2][k] for k in range(3)
-    ]
-    jac_v = [
-        focal_len * inv_depth * turned[1][k] - screen_v * inv_depth * turned[2][k] for k in range(3)
-    ]
+    scale = focal_len * inv_depth
+    screen_u = scale * in_camera[0]
+    screen_v = scale * in_camera[1]
+    slope_u = screen_u * inv_depth
+    slope_v = screen_v * inv_depth
+    jac_u = [scale * turned[0][k] - slope_u * turned[2][k] for k in range(3)]
+    jac_v = [scale * turned[1][k] - slope_v * turned[2][k] for k in range(3)]
     cov_uu = sum((jac_u[k] * jac_u[k] for k in range(3))) + dilation
     cov_uv = sum((jac_u[k] * jac_v[k] for k in range(3)))
     cov_vv = sum((jac_v[k] * jac_v[k] for k in range(3))) + dilation
@@ -113,7 +115,7 @@
 
 def project_block(load, camera):
     params = [load(i) for i in range(11)]
-    feats = geometry(params, camera)
+    feats = screen_conic(params[0:3], shape_axes(*params[3:10]), camera)
     logit = params[10]
     feats.append(jnp.minimum(logit, 0.0) - jnp.log1p(jnp.exp(-jnp.abs(logit))))
     basis = directional(params[0:3], camera)
@@ -151,20 +153,23 @@
 
 
 def order_rows(requests, place):
-    groups, reps = place.shape[:2]
-    place = place.reshape(groups * reps, LANES)
-    lanes = place & (LANES - 1)
-    high = place >> 7
-    result = jnp.zeros_like(place)
-    for r in range(reps):
-        table = jnp.broadcast_to(requests[:, r : r + 1, :], (groups, reps, LANES))
-        picked = lane_pick(table.reshape(groups * reps, LANES), lanes)
-        result = jnp.where(high == r, picked, result)
-    return result.reshape(groups, reps, LANES)
+    cap = place.shape[1]
+    parts = []
+    for c in range(cap // LANES):
+        at = place[:, LANES * c : LANES * c + LANES] & (cap - 1)
+        lanes = at & (LANES - 1)
+        high = at >> 7
+        result = jnp.zeros_like(at)
+        for r in range(cap // LANES):
+            picked = lane_pick(requests[:, LANES * r : LANES * r + LANES], lanes)
+            result = jnp.where(high == r, picked, result)
+        parts.append(result)
+    return parts
 
 
 def order_kernel(request_ref, place_ref, out_ref):
-    out_ref[...] = order_rows(request_ref[...], place_ref[...])
+    for c, part in enumerate(order_rows(request_ref[...], place_ref[...])):
+        out_ref[:, c, :] = part
 
 
 def invert_rows(blocks):
@@ -238,32 +243,41 @@
     out_ref[9 * blocks] = camera_ref[...]
 
 
-def backproject_block(load, cameras, grads, load_out, store_out):
-    params = [load(i) for i in range(11)]
-    kept = [None] * 11
+def backproject_block(load, cameras, grads, store):
+    center = [load(i) for i in range(3)]
+    shaped, back_shape = jax.vjp(shape_axes, *[load(i) for i in range(3, 10)])
+    kept = [0.0] * 12
+    bases = []
+    backs = []
     for v, camera in enumerate(cameras):
-        _, back = jax.vjp(lambda *p: geometry(list(p), camera), *params[0:10])
-        shares = list(back(grads[v][0:5]))
-        basis, back_dir = jax.vjp(lambda *c: directional(list(c), camera), *params[0:3])
-        basis_grads = []
-        for k in range(16):
-            value = 0.0
-            for h in range(3):
-                at = 11 + 3 * k + h
-                scale = sh_zero if k == 0 else basis[k - 1]
-                share = scale * grads[v][6 + h]
-                store_out(at, share if v == 0 else load_out(at) + share)
-                if k:
-                    value = value + load(at) * grads[v][6 + h]
-            if k:
-                basis_grads.append(value)
-        center_shares = back_dir(basis_grads)
-        for i in range(3):
-            shares[i] = shares[i] + center_shares[i]
-        shares.append(grads[v][5] * jax.nn.sigmoid(-params[10]))
-        kept = [s if t is None else t + s for s, t in zip(shares, kept)]
-    for i in range(11):
-        store_out(i, kept[i])
+        _, back = jax.vjp(lambda c, s: screen_conic(c, s, camera), center, shaped)
+        center_grads, shaped_grads = back(grads[v][0:5])
+        shares = list(center_grads) + list(shaped_grads)
+        kept = [t + share for t, share in zip(kept, shares)]
+        basis, back_dir = jax.vjp(lambda *c: directional(list(c), camera), *center)
+        bases.append(basis)
+        backs.append(back_dir)
+    views = range(len(cameras))
+    basis_grads = [[] for _ in views]
+    for k in range(16):
+        for h in range(3):
+            at = 11 + 3 * k + h
+            if k == 0:
+                store(at, sh_zero * sum(grads[v][6 + h] for v in views))
+            else:
+                store(at, sum(bases[v][k - 1] * grads[v][6 + h] for v in views))
+        if k:
+            loaded = [load(11 + 3 * k + h) for h in range(3)]
+            for v in views:
+                basis_grads[v].append(sum(loaded[h] * grads[v][6 + h] for h in range(3)))
+    for v in views:
+        for i, share in enumerate(backs[v](basis_grads[v])):
+            kept[i] = kept[i] + share
+    for i in range(3):
+        store(i, kept[i])
+    for i, share in enumerate(back_shape(kept[3:12])):
+        store(3 + i, share)
+    store(10, sum(grads[v][5] for v in views) * jax.nn.sigmoid(-load(10)))
 
 
 def backproject_kernel(views, blocks, params_ref, grad_ref, out_ref):
@@ -276,7 +290,6 @@
         lambda i: params_ref[i],
         [unpack_camera(grad_ref[v, 9 * blocks]) for v in range(views)],
         [[grad_ref[v, f * blocks + m] for f in range(9)] for v in range(views)],
-        lambda i: out_ref[i],
         store,
     )
 
@@ -292,14 +305,32 @@
     )
 
 
+def turn_block(wide_ref, m, block_ref):
+    width = wide_ref.shape[0]
+    for i in range(0, width, 8):
+        top = min(i + 8, width)
+        for c in range(8):
+            cols = pl.ds(pl.multiple_of(1024 * m + LANES * c, LANES), LANES)
+            block_ref[i:top, c, :] = wide_ref[i:top, cols]
+
+
+def pick_camera(chosen, by_column):
+    index = lax.broadcasted_iota(jnp.int32, by_column.shape, 1)
+    entries = jnp.sum(jnp.where(index == chosen, by_column, 0.0), axis=1, keepdims=True)
+    return jnp.broadcast_to(entries, (by_column.shape[0], LANES))
+
+
 def request_kernel(
     groups,
+    chosen_ref,
     request_ref,
     place_ref,
     params_ref,
-    camera_ref,
+    table_ref,
     arrived_ref,
     inverse_ref,
+    camera_ref,
+    params,
     wanted,
     incoming,
     features,
@@ -321,7 +352,8 @@
         pl.semaphore_signal(
             barrier, inc=1, device_id=(peer(d), view), device_id_type=pl.DeviceIdType.MESH
         )
-    wanted[...] = order_rows(request_ref[...], place_ref[...])
+    for c, part in enumerate(order_rows(request_ref[...], place_ref[...])):
+        wanted[:, c, :] = part
     pl.semaphore_wait(barrier, groups - 1)
 
     asks = []
@@ -334,11 +366,14 @@
         asks.append(ask)
     incoming[me] = wanted[me]
 
-    camera = unpack_camera(camera_ref[...])
+    picked_camera = pick_camera(chosen_ref[0], table_ref[...])
+    camera_ref[...] = picked_camera
+    camera = unpack_camera(picked_camera)
 
     def project(m, carry):
         at = pl.ds(pl.multiple_of(8 * m, 8), 8)
-        feats = project_block(lambda i: params_ref[i, at, :], camera)
+        turn_block(params_ref, m, params)
+        feats = project_block(lambda i: params[i], camera)
         for i in range(9):
             features[i, at, :] = feats[i]
         return carry
@@ -367,18 +402,20 @@
         answer.wait()
 
 
-def request_rows(requests, place, params, camera):
+def request_rows(chosen, requests, place, gaussians, table):
     groups = requests.shape[0]
-    rows = params.shape[1]
+    rows = gaussians.shape[1] // LANES
     return pl.pallas_call(
         functools.partial(request_kernel, groups),
-        in_specs=[VMEM] * 4,
-        out_specs=[VMEM] * 2,
+        in_specs=[pl.BlockSpec(memory_space=pltpu.SMEM)] + [VMEM] * 4,
+        out_specs=[VMEM] * 3,
         out_shape=[
             jax.ShapeDtypeStruct((groups, 9, 8, LANES), F32),
             jax.ShapeDtypeStruct((rows, LANES), jnp.int32),
+            jax.ShapeDtypeStruct((8, LANES), F32),
         ],
         scratch_shapes=[
+            pltpu.VMEM((gaussians.shape[0], 8, LANES), F32),
             pltpu.VMEM((groups, 8, LANES), jnp.int32),
             pltpu.VMEM((groups, 8, LANES), jnp.int32),
             pltpu.VMEM((9, rows, LANES), F32),
@@ -389,7 +426,7 @@
             collective_id=0, has_side_effects=True, vmem_limit_bytes=32 * 1024 * 1024
         ),
         name="request",
-    )(requests, place, params, camera)
+    )(chosen, requests, place, gaussians, table)
 
 
 def return_kernel(
@@ -399,6 +436,8 @@
     camera_ref,
     params_ref,
     out_ref,
+    params,
+    result,
     landed,
     every,
     cameras,
@@ -417,6 +456,7 @@
     diagonal = lax.rem(beside + 2, 4)
     rows = index_ref.shape[0]
     blocks = rows // 8
+    width = params_ref.shape[0]
 
     def peer(d):
         return lax.rem(me + (d + groups), groups)
@@ -473,18 +513,22 @@
     def finish(m, carry):
         ship(0, view, m, beside).wait_recv()
         ship(2, across, m, beside).wait_recv()
-        at = pl.ds(pl.multiple_of(8 * m, 8), 8)
+        turn_block(params_ref, m, params)
 
         def store(i, value):
-            out_ref[i, at, :] = value
+            result[i] = value
 
         backproject_block(
-            lambda i: params_ref[i, at, :],
+            lambda i: params[i],
             [unpack_camera(cameras[v]) for v in range(4)],
             [[every[v, m, f] for f in range(9)] for v in range(4)],
-            lambda i: out_ref[i, at, :],
             store,
         )
+        for i in range(0, width, 8):
+            top = min(i + 8, width)
+            for c in range(8):
+                cols = pl.ds(pl.multiple_of(1024 * m + LANES * c, LANES), LANES)
+                out_ref[i:top, cols] = result[i:top, c, :]
         return carry
 
     lax.fori_loop(0, blocks, finish, 0)
@@ -496,15 +540,17 @@
         ship(2, across, m, beside).wait_send()
 
 
-def return_rows(grads, inverse, camera, params):
+def return_rows(grads, inverse, camera, gaussians):
     groups = grads.shape[0]
-    rows = params.shape[1]
+    rows = gaussians.shape[1] // LANES
     return pl.pallas_call(
         functools.partial(return_kernel, groups),
         in_specs=[VMEM] * 4,
         out_specs=VMEM,
-        out_shape=jax.ShapeDtypeStruct(params.shape, F32),
+        out_shape=jax.ShapeDtypeStruct(gaussians.shape, F32),
         scratch_shapes=[
+            pltpu.VMEM((gaussians.shape[0], 8, LANES), F32),
+            pltpu.VMEM((gaussians.shape[0], 8, LANES), F32),
             pltpu.VMEM((groups, 9, 8, LANES), F32),
             pltpu.VMEM((4, rows // 8, 9, 8, LANES), F32),
             pltpu.VMEM((4, 8, LANES), F32),
@@ -519,7 +565,7 @@
             collective_id=1, has_side_effects=True, vmem_limit_bytes=32 * 1024 * 1024
         ),
         name="return",
-    )(grads, inverse, camera, params)
+    )(grads, inverse, camera, gaussians)
 
 
 def backproject(params, grads):
@@ -583,7 +629,8 @@
 
 def composite_kernel(
     feature_ref,
-    meta_ref,
+    plan_ref,
+    length_ref,
     pixel_grad_ref,
     spread_ref,
     moment_ref,
@@ -602,9 +649,17 @@
 ):
     blocks = feature_ref.shape[0]
     rows = 8 * blocks
-    center_u = meta_ref[0:1, :]
-    center_v = meta_ref[1:2, :]
-    lengths = meta_ref[2:3, :]
+    plan = plan_ref[...].astype(F32)
+    tile_row = jnp.floor((plan + 0.5) * (1.0 / 120.0))
+    tile_column = plan - 120.0 * tile_row
+    copies = LANES // plan.shape[1]
+
+    def on_lanes(value):
+        return jnp.concatenate([value] * copies, axis=1)
+
+    center_u = on_lanes((16.0 * tile_column + 8.0 - 960.0) / HALF)
+    center_v = on_lanes((16.0 * tile_row + 8.0 - 540.0) / HALF)
+    lengths = on_lanes(length_ref[...].astype(F32))
     lane = lax.broadcasted_iota(jnp.int32, (8, LANES), 1)
     sub = lax.broadcasted_iota(jnp.int32, (8, LANES), 0)
 
@@ -655,9 +710,9 @@
 
     def forward(q, carry):
         left, totals = list(carry[0]), list(carry[1])
-        for kk in range(8):
+        for kk in range(16):
             for g in range(2):
-                at = pl.ds(pl.multiple_of(128 * q + 16 * kk + 8 * g, 8), 8)
+                at = pl.ds(pl.multiple_of(256 * q + 16 * kk + 8 * g, 8), 8)
                 colors = [color_ref[at, 128 * h : 128 * h + 128] for h in range(3)]
                 for b in range(2):
                     n = 2 * g + b
@@ -677,20 +732,20 @@
 
     one = jnp.ones((8, LANES), F32)
     zero = jnp.zeros((8, LANES), F32)
-    _, totals = lax.fori_loop(0, rows, forward, ((one,) * 4, (zero,) * 12))
+    _, totals = lax.fori_loop(0, rows // 2, forward, ((one,) * 4, (zero,) * 12))
     for n, (g, b) in enumerate(parts):
         for h in range(3):
-            image_ref[8 * g : 8 * g + 8, h, 128 * b : 128 * b + 128] = totals[3 * n + h]
+            image_ref[16 * h + 8 * g : 16 * h + 8 * g + 8, 128 * b : 128 * b + 128] = totals[3 * n + h]
 
     def sweep(q, behind, stage):
         behind = list(behind)
-        for kk in reversed(range(8)):
+        for kk in reversed(range(16)):
             for b in range(2):
                 cols = slice(128 * b, 128 * b + 128)
                 weights, slopes = [], []
                 for g in range(2):
                     n = 2 * g + b
-                    at = pl.ds(pl.multiple_of(128 * q + 16 * kk + 8 * g, 8), 8)
+                    at = pl.ds(pl.multiple_of(256 * q + 16 * kk + 8 * g, 8), 8)
                     weight = weight_ref[at, cols]
                     gap = shade_ref[at, cols] - behind[n]
                     weights.append(weight)
@@ -703,19 +758,19 @@
         return tuple(behind)
 
     def reduce_stage(q, stage):
-        at = pl.ds(pl.multiple_of(128 * q, 128), 128)
+        at = pl.ds(pl.multiple_of(256 * q, 256), 256)
         sums_ref[at, :] = jnp.dot(stage[...], reduce_ref[...], preferred_element_type=F32)
 
     stage_b[...] = jnp.zeros_like(stage_b)
 
     def backward(i, behind):
-        q = rows - 1 - 2 * i
+        q = rows // 2 - 1 - 2 * i
         reduce_stage(q + 1, stage_b)
         behind = sweep(q, behind, stage_a)
         reduce_stage(q, stage_a)
         return sweep(q - 1, behind, stage_b)
 
-    lax.fori_loop(0, rows // 2, backward, (zero,) * 4)
+    lax.fori_loop(0, rows // 4, backward, (zero,) * 4)
     reduce_stage(0, stage_b)
 
     own = lax.broadcasted_iota(jnp.int32, (16, LANES), 0) == (
@@ -752,15 +807,15 @@
     lax.fori_loop(0, blocks, collect, 0)
 
 
-def composite(features, meta, pixel_grad, tiles):
+def composite(features, plan, lengths, pixel_grad):
     blocks = features.shape[0]
     count = blocks * 8 * LANES
     return pl.pallas_call(
         composite_kernel,
-        in_specs=[VMEM] * 5,
+        in_specs=[VMEM] * 6,
         out_specs=[VMEM] * 2,
         out_shape=[
-            jax.ShapeDtypeStruct((tiles, 3, 256), F32),
+            jax.ShapeDtypeStruct(pixel_grad.shape, F32),
             jax.ShapeDtypeStruct((blocks, 9, 8, LANES), F32),
         ],
         scratch_shapes=[
@@ -770,14 +825,14 @@
             pltpu.VMEM((count, 256), F32),
             pltpu.VMEM((count, 256), F32),
             pltpu.VMEM((1024, LANES), BF16),
-            pltpu.VMEM((128, 1024), BF16),
-            pltpu.VMEM((128, 1024), BF16),
-            pltpu.VMEM((count + 128, LANES), F32),
+            pltpu.VMEM((256, 1024), BF16),
+            pltpu.VMEM((256, 1024), BF16),
+            pltpu.VMEM((count + 256, LANES), F32),
             pltpu.VMEM((9, 8, LANES), F32),
         ],
-        compiler_params=pltpu.CompilerParams(vmem_limit_bytes=56 * 1024 * 1024),
+        compiler_params=pltpu.CompilerParams(vmem_limit_bytes=48 * 1024 * 1024),
         name="composite",
-    )(features, meta, pixel_grad, spread_matrix(), moment_matrix())
+    )(features, plan, lengths, pixel_grad, spread_matrix(), moment_matrix())
 
 
 def to_blocks(sent):
@@ -820,19 +875,21 @@
     rows = slots // LANES
     blocks = rows // 8
 
-    chosen = (jnp.arange(camera_table.shape[0], dtype=jnp.int32) == view_camera[0]).astype(F32)
-    camera = jnp.sum(camera_table * chosen[:, None], axis=0)
-    camera = jnp.broadcast_to(camera[:, None], (8, LANES))
-    params = gaussians.reshape(gaussians.shape[0], rows, LANES)
-
-    base = jnp.arange(groups, dtype=jnp.int32)[:, None] * cap
-    place = (tile_lists[0].T.reshape(groups, cap) - base).reshape(groups, reps, LANES)
-    asked = requests[0, 0].reshape(groups, reps, LANES)
+    place = tile_lists[0].T.reshape(groups, cap)
+    asked = requests[0, 0]
     fused = reps == 8 and rows == 8 * groups and views == 4
     if fused:
-        arrived, inverse = request_rows(asked, place, params, camera)
+        arrived, inverse, camera = request_rows(
+            view_camera, asked, place, gaussians, camera_table.T
+        )
     else:
-        wanted = simple_call(order_kernel, place.shape, jnp.int32, "order", asked, place)
+        params = gaussians.reshape(gaussians.shape[0], rows, LANES)
+        chosen = (jnp.arange(camera_table.shape[0], dtype=jnp.int32) == view_camera[0]).astype(F32)
+        camera = jnp.sum(camera_table * chosen[:, None], axis=0)
+        camera = jnp.broadcast_to(camera[:, None], (8, LANES))
+        wanted = simple_call(
+            order_kernel, (groups, reps, LANES), jnp.int32, "order", asked, place
+        )
         incoming = exchange(wanted).reshape(groups * reps, LANES)
         features = project_all(params, camera)
         sent = simple_call(
@@ -841,23 +898,19 @@
         arrived = to_blocks(exchange(from_blocks(sent, groups, reps)))
         inverse = simple_call(invert_kernel, (rows, LANES), jnp.int32, "invert", incoming)
 
-    plan = tile_plan[0]
-    center_u = ((plan % 120 * 16 + 8).astype(F32) - 960.0) / HALF
-    center_v = ((plan // 120 * 16 + 8).astype(F32) - 540.0) / HALF
-    meta = jnp.stack([center_u, center_v, tile_lengths[0].astype(F32)])
-    meta = jnp.tile(meta, (1, LANES // tiles))
     by_color = pixel_grad[0].transpose(1, 0, 2).reshape(3 * tiles, 256)
-    image, row_grads = composite(arrived, meta, by_color, tiles)
+    image, row_grads = composite(arrived, tile_plan, tile_lengths, by_color)
+    image = image.reshape(3, tiles, 256).transpose(1, 0, 2)
 
     if fused:
-        total = return_rows(row_grads, inverse, camera, params)
+        total = return_rows(row_grads, inverse, camera, gaussians)
     else:
         returned = to_blocks(exchange(from_blocks(row_grads, groups, reps)))
         packed = simple_call(
             ungather_kernel, (9 * blocks + 1, 8, LANES), F32, "ungather", returned, inverse, camera
         )
-        total = backproject(params, lax.all_gather(packed, "view"))
-    return (image[None], total.reshape(gaussians.shape))
+        total = backproject(params, lax.all_gather(packed, "view")).reshape(gaussians.shape)
+    return (image[None], total)
 
 
 def solution(mesh):

time: 92.2 us -> 85.1 us (0.923)
  local copies, waits for them, and re-layouts: 10.6 us -> 5.42 us
  Pallas kernels: 79.6 us -> 77.8 us
    unnamed x15 -> x19, local copies, waits for them, and re-layouts: 8.61 us -> 4.38 us
    pallas_call x2, Pallas kernels: 52.2 us -> 49.1 us  [the longest x1 29.1 us: composite(): pl.pallas_call(composite_kernel, in_specs=[VMEM] * 6, out_specs=[VMEM] *...]
    pallas_call x1, Pallas kernels: 27.4 us -> 28.7 us  [return_rows(): pl.pallas_call(functools.partial(return_kernel, groups), in_specs=[VMEM]...]
where the time goes in v3:
time: 85.1 us; the launch traced here: 84.7 us
  Pallas kernels  77.8 us (91%)
  local copies, waits for them, and re-layouts  5.42 us (6%)
  between operations  1.45 us (2%)
    pallas_call x1, Pallas kernels, composite(): pl.pallas_call(composite_kernel, in_specs=[VMEM] * 6, out_specs=[VMEM] *...  29.1 us
    pallas_call x1, Pallas kernels, return_rows(): pl.pallas_call(functools.partial(return_kernel, groups), in_specs=[VMEM]...  28.7 us
    pallas_call x1, Pallas kernels, request_rows(): pl.pallas_call(functools.partial(request_kernel, groups), in_specs=[pl.Bl...  20 us
    unnamed x19, local copies, waits for them, and re-layouts  4.38 us

profile of v3, /device:TPU:0, one launch (start us, length us, event | category | flops | bytes accessed | tf_op | source)
XLA Modules:
  0.0 84.7 jit_solution(8094407350861690396)
XLA Ops:
  0.6 0.0 copy-start.2
  0.6 0.0 copy-start.4
  0.7 0.0 copy-start.3
  0.7 0.0 copy-start.8
  0.7 0.0 copy-start.7
  1.4 0.9 %copy.13 = s32[512,16]{1,0:T(8,128)S(1)} copy(s32[512,16]{0,1:T(8,128)} %bitcast.18) | data formatting | bytes 65536 | tf_op jit(solution)/shard_map/transpose | solution.py:878
  2.3 0.2 reshape.13.place_ref
  2.4 0.0 copy-start
  2.4 1.6 %copy-done = f32[59,8192]{1,0:T(8,128)S(1)} copy-done((f32[59,8192]{1,0:T(8,128)S(1)}, f32[59,8192]{1,0:T(8,128)}, u32[]{:S(2)}) %copy-start) | copy-done | bytes 1933336
  4.0 0.0 copy-start.5
  4.0 0.8 copy-done.5
  4.8 0.0 copy-start.6
  4.8 0.7 copy-done.6
  5.5 0.0 copy-start.1
  5.5 20.0 %request.1 = (f32[8,9,8,128]{3,2,1,0:T(8,128)S(1)}, s32[64,128]{1,0:T(8,128)S(1)}, f32[8,128]{1,0:T(8,128)S(1)}) custom-call(s32[1]{0:T(128)S(6)} %copy.15.chosen_ref, s32[8,1024]{1,0:T(8,128)S(1)} %bitcast.16, s32[8,1024]{1,0:T(8,128)S(1)} %reshape.13.place_ref, f32[59,8192]{1,0:T(8,128)S(1)} %copy-done, f32[8,16]{1,0:T(8,128)S(1)} %bitcast.17), custom_call_target="tpu_custom_call" | custom-call | tf_op jit(solution)/shard_map/request/pallas_call | solution.py:408
  25.5 0.0 copy-done.2
  25.5 0.0 copy-done.4
  25.5 0.0 copy-done.3
  25.5 0.0 copy-done.8
  25.6 0.0 copy-done.7
  25.6 29.1 %composite.1 = (f32[48,256]{1,0:T(8,128)}, f32[8,9,8,128]{3,2,1,0:T(8,128)S(1)}) custom-call(f32[8,9,8,128]{3,2,1,0:T(8,128)S(1)} %get-tuple-element.7.feature_ref, s32[1,16]{1,0:T(1,128)S(1)} %copy-done.7, s32[1,16]{1,0:T(1,128)S(1)} %copy-done.8, f32[48,256]{1,0:T(8,128)S(1)} %bitcast.15, bf16[32,640]{1,0:T(8,128)(2,1)S(1)} %copy-done.4, ...), custom_call_target="tpu_custom_call" | custom-call | tf_op jit(solution)/shard_map/composite/pallas_call | solution.py:813
  54.7 0.0 copy-done.1
  54.7 28.7 %return.1 = f32[59,8192]{1,0:T(8,128)S(1)} custom-call(f32[8,9,8,128]{3,2,1,0:T(8,128)S(1)} %get-tuple-element.9.grad_ref, s32[64,128]{1,0:T(8,128)S(1)} %get-tuple-element.10.index_ref, f32[8,128]{1,0:T(8,128)S(1)} %get-tuple-element.11.camera_ref, f32[59,8192]{1,0:T(8,128)S(1)} %copy-done.1), custom_call_target="tpu_custom_call" | custom-call | tf_op jit(solution)/shard_map/return/pallas_call | solution.py:546
  83.4 1.3 %copy.16 = f32[59,8192]{1,0:T(8,128)} copy(f32[59,8192]{1,0:T(8,128)S(1)} %return.1) | data formatting | bytes 3866624
Async XLA Ops:
  0.6 24.9 %copy-start.2 = (bf16[256,128]{1,0:T(8,128)(2,1)S(1)}, bf16[256,128]{1,0:T(8,128)(2,1)}, u32[]{:S(2)}) copy-start(bf16[256,128]{1,0:T(8,128)(2,1)} %constant.5.clone.moment_ref) | copy-start | bytes 196612
  0.6 24.9 %copy-start.4 = (bf16[32,640]{1,0:T(8,128)(2,1)S(1)}, bf16[32,640]{1,0:T(8,128)(2,1)}, u32[]{:S(2)}) copy-start(bf16[32,640]{1,0:T(8,128)(2,1)} %constant.4.clone.spread_ref) | copy-start | bytes 122884
  0.7 24.9 %copy-start.3 = (f32[1,16,3,256]{3,1,2,0:T(8,128)S(1)}, f32[1,16,3,256]{3,1,2,0:T(8,128)}, u32[]{:S(2)}) copy-start(f32[1,16,3,256]{3,1,2,0:T(8,128)} %param.17) | copy-start | bytes 147460
  0.7 24.9 %copy-start.8 = (s32[1,16]{1,0:T(1,128)S(1)}, s32[1,16]{1,0:T(1,128)}, u32[]{:S(2)}) copy-start(s32[1,16]{1,0:T(1,128)} %length_ref.1) | copy-start | bytes 196
  0.7 24.9 %copy-start.7 = (s32[1,16]{1,0:T(1,128)S(1)}, s32[1,16]{1,0:T(1,128)}, u32[]{:S(2)}) copy-start(s32[1,16]{1,0:T(1,128)} %plan_ref.1) | copy-start | bytes 196
  2.4 1.6 %copy-start = (f32[59,8192]{1,0:T(8,128)S(1)}, f32[59,8192]{1,0:T(8,128)}, u32[]{:S(2)}) copy-start(f32[59,8192]{1,0:T(8,128)} %params_ref.3) | copy-start | bytes 5799940
  4.0 0.8 copy-start.5
  4.8 0.7 copy-start.6
  5.5 49.2 %copy-start.1 = (f32[59,8192]{1,0:T(8,128)S(1)}, f32[59,8192]{1,0:T(8,128)}, u32[]{:S(2)}) copy-start(f32[59,8192]{1,0:T(8,128)} %params_ref.3) | copy-start | bytes 5799940

commit v4 on v3

--- a/solution.py
+++ b/solution.py
@@ -211,6 +211,34 @@
 
     start = tuple(jnp.zeros((8, LANES), F32) for _ in range(9))
     return lax.fori_loop(0, source_rows, step, start, unroll=8)
+
+
+def fill_table(load, table_ref):
+    for f in range(9):
+        for s, part in enumerate(split_three(load(f))):
+            turned = jnp.transpose(part)
+            table_ref[64 * f : 64 * f + 64, 128 * s : 128 * s + 128] = jnp.concatenate(
+                [turned[:64], turned[64:]], axis=1
+            ).astype(BF16)
+
+
+def table_pick(table_ref, index, store):
+    high_iota = lax.broadcasted_iota(jnp.int32, (128, 256), 0)
+    low_iota = lax.broadcasted_iota(jnp.int32, (64, 256), 0)
+    for c in range(4):
+        slot = jnp.concatenate([index[2 * c : 2 * c + 1], index[2 * c + 1 : 2 * c + 2]], axis=1)
+        high = ((slot >> 6) & 1) * 64 + (slot >> 7)
+        hit = jnp.where(high_iota == high, 1.0, 0.0).astype(BF16)
+        found = jnp.dot(
+            table_ref[...], jnp.concatenate([hit] * 3, axis=0), preferred_element_type=F32
+        )
+        own = low_iota == (slot & 63)
+        for f in range(9):
+            row = jnp.sum(
+                jnp.where(own, found[64 * f : 64 * f + 64], 0.0), axis=0, keepdims=True
+            )
+            store(f, 2 * c, row[:, :LANES])
+            store(f, 2 * c + 1, row[:, LANES:])
 
 
 def gather_kernel(feature_ref, index_ref, out_ref):
@@ -334,6 +362,7 @@
     wanted,
     incoming,
     features,
+    table,
     outbox,
     ask_send,
     ask_recv,
@@ -380,26 +409,44 @@
 
     lax.fori_loop(0, rows // 8, project, 0)
 
-    answers = []
-    for d in range(groups):
-        if d:
-            asks[d - 1].wait_recv()
-        to = peer(-d)
-        picked = pick_block(lambda f, r: features[f, pl.ds(r, 1), :], incoming[to], rows)
-        box = outbox.at[d] if d else arrived_ref.at[me]
-        for f in range(9):
-            box[f] = picked[f]
-        if d:
-            answer = remote(
-                outbox.at[d], arrived_ref.at[me], row_send.at[d], row_recv.at[d], (to, view)
-            )
-            answer.start()
-            answers.append(answer)
+    fill_table(lambda f: features[f], table)
+
+    def ask_of(d):
+        to = peer(d)
+        return remote(
+            wanted.at[to], incoming.at[me], ask_send.at[d], ask_recv.at[d], (to, view)
+        )
+
+    def answer_of(d):
+        return remote(
+            outbox.at[d],
+            arrived_ref.at[me],
+            row_send.at[d],
+            row_recv.at[d],
+            (peer(-d), view),
+        )
+
+    def answer(d, carry):
+        ask_of(d).wait_recv()
+
+        def store(f, r, values):
+            outbox[d, f, r : r + 1, :] = values
+
+        table_pick(table, incoming[peer(-d)], store)
+        answer_of(d).start()
+        return carry
+
+    lax.fori_loop(1, groups, answer, 0)
+
+    def store_own(f, r, values):
+        arrived_ref[me, f, r : r + 1, :] = values
+
+    table_pick(table, incoming[me], store_own)
     inverse_ref[...] = invert_rows([incoming[s] for s in range(groups)])
     for ask in asks:
         ask.wait_send()
-    for answer in answers:
-        answer.wait()
+    for d in range(1, groups):
+        answer_of(d).wait()
 
 
 def request_rows(chosen, requests, place, gaussians, table):
@@ -419,6 +466,7 @@
             pltpu.VMEM((groups, 8, LANES), jnp.int32),
             pltpu.VMEM((groups, 8, LANES), jnp.int32),
             pltpu.VMEM((9, rows, LANES), F32),
+            pltpu.VMEM((576, 384), BF16),
             pltpu.VMEM((groups, 9, 8, LANES), F32),
         ]
         + [pltpu.SemaphoreType.DMA((groups,))] * 4,
@@ -438,6 +486,7 @@
     out_ref,
     params,
     result,
+    table,
     landed,
     every,
     cameras,
@@ -497,16 +546,25 @@
         ship(1, view, m, across).wait_recv()
         ship(2, across, m, beside).start()
 
-    for m in range(blocks):
-        picked = pick_block(
-            lambda f, r: landed[r // 8, f, pl.ds(r % 8, 1), :], index_ref[8 * m : 8 * m + 8, :], rows
-        )
-        for f in range(9):
-            every[view, m, f] = picked[f]
+    fill_table(
+        lambda f: jnp.concatenate([landed[o, f] for o in range(groups)], axis=0), table
+    )
+
+    def spread(m, carry):
+        def store(f, r, values):
+            every[view, m, f, r : r + 1, :] = values
+
+        table_pick(table, index_ref[pl.ds(pl.multiple_of(8 * m, 8), 8), :], store)
         ship(0, view, m, beside).start()
         ship(1, view, m, across).start()
-        if m >= 2:
+
+        @pl.when(m >= 2)
+        def _():
             forward(m - 2)
+
+        return carry
+
+    lax.fori_loop(0, blocks, spread, 0)
     for m in range(blocks - 2, blocks):
         forward(m)
 
@@ -551,6 +609,7 @@
         scratch_shapes=[
             pltpu.VMEM((gaussians.shape[0], 8, LANES), F32),
             pltpu.VMEM((gaussians.shape[0], 8, LANES), F32),
+            pltpu.VMEM((576, 384), BF16),
             pltpu.VMEM((groups, 9, 8, LANES), F32),
             pltpu.VMEM((4, rows // 8, 9, 8, LANES), F32),
             pltpu.VMEM((4, 8, LANES), F32),
@@ -877,7 +936,7 @@
 
     place = tile_lists[0].T.reshape(groups, cap)
     asked = requests[0, 0]
-    fused = reps == 8 and rows == 8 * groups and views == 4
+    fused = reps == 8 and rows == 64 and groups == 8 and views == 4
     if fused:
         arrived, inverse, camera = request_rows(
             view_camera, asked, place, gaussians, camera_table.T

time: 85.1 us -> 82.5 us (0.969)
  Pallas kernels: 77.8 us -> 75.3 us
    pallas_call x1, Pallas kernels: 20 us -> 18.3 us  [request_rows(): pl.pallas_call(functools.partial(request_kernel, groups), in_specs=[pl.Bl...]
where the time goes in v4:
time: 82.5 us; the launch traced here: 82.1 us
  Pallas kernels  75.3 us (91%)
  local copies, waits for them, and re-layouts  5.42 us (7%)
  between operations  1.45 us (2%)
    pallas_call x1, Pallas kernels, composite(): pl.pallas_call(composite_kernel, in_specs=[VMEM] * 6, out_specs=[VMEM] *...  29.1 us
    pallas_call x1, Pallas kernels, return_rows(): pl.pallas_call(functools.partial(return_kernel, groups), in_specs=[VMEM]...  27.9 us
    pallas_call x1, Pallas kernels, request_rows(): pl.pallas_call(functools.partial(request_kernel, groups), in_specs=[pl.Bl...  18.3 us
    unnamed x19, local copies, waits for them, and re-layouts  4.38 us

profile of v4, /device:TPU:0, one launch (start us, length us, event | category | flops | bytes accessed | tf_op | source)
XLA Modules:
  0.0 82.1 jit_solution(3601144733637212611)
XLA Ops:
  0.6 0.0 copy-start.2
  0.6 0.0 copy-start.4
  0.7 0.0 copy-start.3
  0.7 0.0 copy-start.8
  0.7 0.0 copy-start.7
  1.4 0.9 %copy.13 = s32[512,16]{1,0:T(8,128)S(1)} copy(s32[512,16]{0,1:T(8,128)} %bitcast.18) | data formatting | bytes 65536 | tf_op jit(solution)/shard_map/transpose | solution.py:937
  2.3 0.2 reshape.13.place_ref
  2.4 0.0 copy-start
  2.4 1.6 %copy-done = f32[59,8192]{1,0:T(8,128)S(1)} copy-done((f32[59,8192]{1,0:T(8,128)S(1)}, f32[59,8192]{1,0:T(8,128)}, u32[]{:S(2)}) %copy-start) | copy-done | bytes 1933336
  4.0 0.0 copy-start.5
  4.0 0.8 copy-done.5
  4.8 0.0 copy-start.6
  4.8 0.7 copy-done.6
  5.5 0.0 copy-start.1
  5.5 18.3 %request.1 = (f32[8,9,8,128]{3,2,1,0:T(8,128)S(1)}, s32[64,128]{1,0:T(8,128)S(1)}, f32[8,128]{1,0:T(8,128)S(1)}) custom-call(s32[1]{0:T(128)S(6)} %copy.15.chosen_ref, s32[8,1024]{1,0:T(8,128)S(1)} %bitcast.16, s32[8,1024]{1,0:T(8,128)S(1)} %reshape.13.place_ref, f32[59,8192]{1,0:T(8,128)S(1)} %copy-done, f32[8,16]{1,0:T(8,128)S(1)} %bitcast.17), custom_call_target="tpu_custom_call" | custom-call | tf_op jit(solution)/shard_map/request/pallas_call | solution.py:455
  23.7 0.0 copy-done.2
  23.7 0.0 copy-done.4
  23.8 0.0 copy-done.3
  23.8 0.0 copy-done.8
  23.8 0.0 copy-done.7
  23.8 29.1 %composite.1 = (f32[48,256]{1,0:T(8,128)}, f32[8,9,8,128]{3,2,1,0:T(8,128)S(1)}) custom-call(f32[8,9,8,128]{3,2,1,0:T(8,128)S(1)} %get-tuple-element.7.feature_ref, s32[1,16]{1,0:T(1,128)S(1)} %copy-done.7, s32[1,16]{1,0:T(1,128)S(1)} %copy-done.8, f32[48,256]{1,0:T(8,128)S(1)} %bitcast.15, bf16[32,640]{1,0:T(8,128)(2,1)S(1)} %copy-done.4, ...), custom_call_target="tpu_custom_call" | custom-call | tf_op jit(solution)/shard_map/composite/pallas_call | solution.py:872
  52.9 0.0 copy-done.1
  52.9 27.9 %return.1 = f32[59,8192]{1,0:T(8,128)S(1)} custom-call(f32[8,9,8,128]{3,2,1,0:T(8,128)S(1)} %get-tuple-element.9.grad_ref, s32[64,128]{1,0:T(8,128)S(1)} %get-tuple-element.10.index_ref, f32[8,128]{1,0:T(8,128)S(1)} %get-tuple-element.11.camera_ref, f32[59,8192]{1,0:T(8,128)S(1)} %copy-done.1), custom_call_target="tpu_custom_call" | custom-call | tf_op jit(solution)/shard_map/return/pallas_call | solution.py:604
  80.8 1.3 %copy.16 = f32[59,8192]{1,0:T(8,128)} copy(f32[59,8192]{1,0:T(8,128)S(1)} %return.1) | data formatting | bytes 3866624
Async XLA Ops:
  0.6 23.1 %copy-start.2 = (bf16[256,128]{1,0:T(8,128)(2,1)S(1)}, bf16[256,128]{1,0:T(8,128)(2,1)}, u32[]{:S(2)}) copy-start(bf16[256,128]{1,0:T(8,128)(2,1)} %constant.5.clone.moment_ref) | copy-start | bytes 196612
  0.6 23.1 %copy-start.4 = (bf16[32,640]{1,0:T(8,128)(2,1)S(1)}, bf16[32,640]{1,0:T(8,128)(2,1)}, u32[]{:S(2)}) copy-start(bf16[32,640]{1,0:T(8,128)(2,1)} %constant.4.clone.spread_ref) | copy-start | bytes 122884
  0.7 23.1 %copy-start.3 = (f32[1,16,3,256]{3,1,2,0:T(8,128)S(1)}, f32[1,16,3,256]{3,1,2,0:T(8,128)}, u32[]{:S(2)}) copy-start(f32[1,16,3,256]{3,1,2,0:T(8,128)} %param.17) | copy-start | bytes 147460
  0.7 23.1 %copy-start.8 = (s32[1,16]{1,0:T(1,128)S(1)}, s32[1,16]{1,0:T(1,128)}, u32[]{:S(2)}) copy-start(s32[1,16]{1,0:T(1,128)} %length_ref.1) | copy-start | bytes 196
  0.7 23.1 %copy-start.7 = (s32[1,16]{1,0:T(1,128)S(1)}, s32[1,16]{1,0:T(1,128)}, u32[]{:S(2)}) copy-start(s32[1,16]{1,0:T(1,128)} %plan_ref.1) | copy-start | bytes 196
  2.4 1.6 %copy-start = (f32[59,8192]{1,0:T(8,128)S(1)}, f32[59,8192]{1,0:T(8,128)}, u32[]{:S(2)}) copy-start(f32[59,8192]{1,0:T(8,128)} %params_ref.3) | copy-start | bytes 5799940
  4.0 0.8 copy-start.5
  4.8 0.7 copy-start.6
  5.5 47.4 %copy-start.1 = (f32[59,8192]{1,0:T(8,128)S(1)}, f32[59,8192]{1,0:T(8,128)}, u32[]{:S(2)}) copy-start(f32[59,8192]{1,0:T(8,128)} %params_ref.3) | copy-start | bytes 5799940

commit v5 on v4

--- a/solution.py
+++ b/solution.py
@@ -696,8 +696,11 @@
     image_ref,
     out_ref,
     coef_ref,
+    power_a,
+    power_b,
+    color_a,
+    color_b,
     alpha_ref,
-    color_ref,
     weight_ref,
     shade_ref,
     reduce_ref,
@@ -748,17 +751,15 @@
     reduce_ref[512:768, :] = moment_ref[...]
     reduce_ref[768:1024, :] = moment_ref[...]
 
-    def expand(i, carry):
+    coef_ref[rows : rows + 2] = jnp.zeros((2, 32, LANES), F32)
+
+    def expand(q, power, color):
         left = jnp.concatenate(
-            [jnp.transpose(coef_ref[4 * i + s]) for s in range(4)], axis=0
+            [jnp.transpose(coef_ref[2 * q + s]) for s in range(2)], axis=0
         ).astype(BF16)
         spread = jnp.dot(left, spread_ref[...], preferred_element_type=F32)
-        at = pl.ds(pl.multiple_of(512 * i, 512), 512)
-        alpha_ref[at, :] = spread[:, 0:256]
-        color_ref[at, :] = spread[:, 256:640]
-        return carry
-
-    lax.fori_loop(0, rows // 4, expand, 0)
+        power[...] = spread[:, 0:256]
+        color[...] = spread[:, 256:640]
 
     parts = [(g, b) for g in range(2) for b in range(2)]
     pixel_grads = {
@@ -767,16 +768,17 @@
         for h in range(3)
     }
 
-    def forward(q, carry):
+    def forward(q, carry, power, color):
         left, totals = list(carry[0]), list(carry[1])
         for kk in range(16):
             for g in range(2):
                 at = pl.ds(pl.multiple_of(256 * q + 16 * kk + 8 * g, 8), 8)
-                colors = [color_ref[at, 128 * h : 128 * h + 128] for h in range(3)]
+                near = slice(16 * kk + 8 * g, 16 * kk + 8 * g + 8)
+                colors = [color[near, 128 * h : 128 * h + 128] for h in range(3)]
                 for b in range(2):
                     n = 2 * g + b
                     cols = slice(128 * b, 128 * b + 128)
-                    alpha = jnp.exp2(alpha_ref[at, cols])
+                    alpha = jnp.exp2(power[near, cols])
                     weight = alpha * left[n]
                     left[n] = left[n] - weight
                     shade = colors[0] * pixel_grads[g, b, 0]
@@ -791,7 +793,15 @@
 
     one = jnp.ones((8, LANES), F32)
     zero = jnp.zeros((8, LANES), F32)
-    _, totals = lax.fori_loop(0, rows // 2, forward, ((one,) * 4, (zero,) * 12))
+    expand(0, power_a, color_a)
+
+    def two_forward(i, carry):
+        expand(2 * i + 1, power_b, color_b)
+        carry = forward(2 * i, carry, power_a, color_a)
+        expand(2 * i + 2, power_a, color_a)
+        return forward(2 * i + 1, carry, power_b, color_b)
+
+    _, totals = lax.fori_loop(0, rows // 4, two_forward, ((one,) * 4, (zero,) * 12))
     for n, (g, b) in enumerate(parts):
         for h in range(3):
             image_ref[16 * h + 8 * g : 16 * h + 8 * g + 8, 128 * b : 128 * b + 128] = totals[3 * n + h]
@@ -878,9 +888,12 @@
             jax.ShapeDtypeStruct((blocks, 9, 8, LANES), F32),
         ],
         scratch_shapes=[
-            pltpu.VMEM((8 * blocks, 32, LANES), F32),
+            pltpu.VMEM((8 * blocks + 2, 32, LANES), F32),
+            pltpu.VMEM((256, 256), F32),
+            pltpu.VMEM((256, 256), F32),
+            pltpu.VMEM((256, 384), F32),
+            pltpu.VMEM((256, 384), F32),
             pltpu.VMEM((count, 256), F32),
-            pltpu.VMEM((count, 384), F32),
             pltpu.VMEM((count, 256), F32),
             pltpu.VMEM((count, 256), F32),
             pltpu.VMEM((1024, LANES), BF16),

time: 82.5 us -> 74 us (0.90)
  Pallas kernels: 75.3 us -> 66.8 us
    pallas_call x1, Pallas kernels: 29.1 us -> 20.6 us  [composite(): pl.pallas_call(composite_kernel, in_specs=[VMEM] * 6, out_specs=[VMEM] *...]
where the time goes in v5:
time: 74 us; the launch traced here: 73.6 us
  Pallas kernels  66.8 us (90%)
  local copies, waits for them, and re-layouts  5.42 us (7%)
  between operations  1.45 us (2%)
    pallas_call x1, Pallas kernels, return_rows(): pl.pallas_call(functools.partial(return_kernel, groups), in_specs=[VMEM]...  27.9 us
    pallas_call x1, Pallas kernels, composite(): pl.pallas_call(composite_kernel, in_specs=[VMEM] * 6, out_specs=[VMEM] *...  20.6 us
    pallas_call x1, Pallas kernels, request_rows(): pl.pallas_call(functools.partial(request_kernel, groups), in_specs=[pl.Bl...  18.3 us
    unnamed x19, local copies, waits for them, and re-layouts  4.38 us

profile of v5, /device:TPU:0, one launch (start us, length us, event | category | flops | bytes accessed | tf_op | source)
XLA Modules:
  0.0 73.6 jit_solution(4776335314452236181)
XLA Ops:
  0.6 0.0 copy-start.2
  0.6 0.0 copy-start.4
  0.7 0.0 copy-start.3
  0.7 0.0 copy-start.8
  0.7 0.0 copy-start.7
  1.4 0.9 %copy.13 = s32[512,16]{1,0:T(8,128)S(1)} copy(s32[512,16]{0,1:T(8,128)} %bitcast.18) | data formatting | bytes 65536 | tf_op jit(solution)/shard_map/transpose | solution.py:950
  2.3 0.2 reshape.13.place_ref
  2.4 0.0 copy-start
  2.4 1.6 %copy-done = f32[59,8192]{1,0:T(8,128)S(1)} copy-done((f32[59,8192]{1,0:T(8,128)S(1)}, f32[59,8192]{1,0:T(8,128)}, u32[]{:S(2)}) %copy-start) | copy-done | bytes 1933336
  4.0 0.0 copy-start.5
  4.0 0.8 %copy-done.5 = s32[1,1,8,1024]{3,2,1,0:T(8,128)S(1)} copy-done((s32[1,1,8,1024]{3,2,1,0:T(8,128)S(1)}, s32[1,1,8,1024]{3,2,1,0:T(8,128)}, u32[]{:S(2)}) %copy-start.5) | copy-done | bytes 32792
  4.8 0.0 copy-start.6
  4.8 0.7 copy-done.6
  5.5 0.0 copy-start.1
  5.5 18.3 %request.1 = (f32[8,9,8,128]{3,2,1,0:T(8,128)S(1)}, s32[64,128]{1,0:T(8,128)S(1)}, f32[8,128]{1,0:T(8,128)S(1)}) custom-call(s32[1]{0:T(128)S(6)} %copy.15.chosen_ref, s32[8,1024]{1,0:T(8,128)S(1)} %bitcast.16, s32[8,1024]{1,0:T(8,128)S(1)} %reshape.13.place_ref, f32[59,8192]{1,0:T(8,128)S(1)} %copy-done, f32[8,16]{1,0:T(8,128)S(1)} %bitcast.17), custom_call_target="tpu_custom_call" | custom-call | tf_op jit(solution)/shard_map/request/pallas_call | solution.py:455
  23.7 0.0 copy-done.2
  23.7 0.0 copy-done.4
  23.8 0.0 copy-done.3
  23.8 0.0 copy-done.8
  23.8 0.0 copy-done.7
  23.8 20.6 %composite.1 = (f32[48,256]{1,0:T(8,128)}, f32[8,9,8,128]{3,2,1,0:T(8,128)S(1)}) custom-call(f32[8,9,8,128]{3,2,1,0:T(8,128)S(1)} %get-tuple-element.7.feature_ref, s32[1,16]{1,0:T(1,128)S(1)} %copy-done.7, s32[1,16]{1,0:T(1,128)S(1)} %copy-done.8, f32[48,256]{1,0:T(8,128)S(1)} %bitcast.15, bf16[32,640]{1,0:T(8,128)(2,1)S(1)} %copy-done.4, ...), custom_call_target="tpu_custom_call" | custom-call | tf_op jit(solution)/shard_map/composite/pallas_call | solution.py:882
  44.4 0.0 copy-done.1
  44.4 27.9 %return.1 = f32[59,8192]{1,0:T(8,128)S(1)} custom-call(f32[8,9,8,128]{3,2,1,0:T(8,128)S(1)} %get-tuple-element.9.grad_ref, s32[64,128]{1,0:T(8,128)S(1)} %get-tuple-element.10.index_ref, f32[8,128]{1,0:T(8,128)S(1)} %get-tuple-element.11.camera_ref, f32[59,8192]{1,0:T(8,128)S(1)} %copy-done.1), custom_call_target="tpu_custom_call" | custom-call | tf_op jit(solution)/shard_map/return/pallas_call | solution.py:604
  72.3 1.3 %copy.16 = f32[59,8192]{1,0:T(8,128)} copy(f32[59,8192]{1,0:T(8,128)S(1)} %return.1) | data formatting | bytes 3866624
Async XLA Ops:
  0.6 23.1 %copy-start.2 = (bf16[256,128]{1,0:T(8,128)(2,1)S(1)}, bf16[256,128]{1,0:T(8,128)(2,1)}, u32[]{:S(2)}) copy-start(bf16[256,128]{1,0:T(8,128)(2,1)} %constant.5.clone.moment_ref) | copy-start | bytes 196612
  0.6 23.1 %copy-start.4 = (bf16[32,640]{1,0:T(8,128)(2,1)S(1)}, bf16[32,640]{1,0:T(8,128)(2,1)}, u32[]{:S(2)}) copy-start(bf16[32,640]{1,0:T(8,128)(2,1)} %constant.4.clone.spread_ref) | copy-start | bytes 122884
  0.7 23.1 %copy-start.3 = (f32[1,16,3,256]{3,1,2,0:T(8,128)S(1)}, f32[1,16,3,256]{3,1,2,0:T(8,128)}, u32[]{:S(2)}) copy-start(f32[1,16,3,256]{3,1,2,0:T(8,128)} %param.17) | copy-start | bytes 147460
  0.7 23.1 %copy-start.8 = (s32[1,16]{1,0:T(1,128)S(1)}, s32[1,16]{1,0:T(1,128)}, u32[]{:S(2)}) copy-start(s32[1,16]{1,0:T(1,128)} %length_ref.1) | copy-start | bytes 196
  0.7 23.1 %copy-start.7 = (s32[1,16]{1,0:T(1,128)S(1)}, s32[1,16]{1,0:T(1,128)}, u32[]{:S(2)}) copy-start(s32[1,16]{1,0:T(1,128)} %plan_ref.1) | copy-start | bytes 196
  2.4 1.6 %copy-start = (f32[59,8192]{1,0:T(8,128)S(1)}, f32[59,8192]{1,0:T(8,128)}, u32[]{:S(2)}) copy-start(f32[59,8192]{1,0:T(8,128)} %params_ref.3) | copy-start | bytes 5799940
  4.0 0.8 %copy-start.5 = (s32[1,1,8,1024]{3,2,1,0:T(8,128)S(1)}, s32[1,1,8,1024]{3,2,1,0:T(8,128)}, u32[]{:S(2)}) copy-start(s32[1,1,8,1024]{3,2,1,0:T(8,128)} %param.14) | copy-start | bytes 98308
  4.8 0.7 copy-start.6
  5.5 38.9 %copy-start.1 = (f32[59,8192]{1,0:T(8,128)S(1)}, f32[59,8192]{1,0:T(8,128)}, u32[]{:S(2)}) copy-start(f32[59,8192]{1,0:T(8,128)} %params_ref.3) | copy-start | bytes 5799940
